TPU v7x, 32 devices: a whole 2x2x4 slice. The times are simulated.
32 devices in a mesh: blk: 8 (over z, core), grp: 4 (over y, x).
Axes of the slice: x: 2, y: 2, z: 4, core: 2. Of those that a mesh axis runs over, the one named last changes fastest.
Arguments:
- queries: bfloat16 [64, 5120], P(('grp', 'blk')), parts along dimension 0, may hold values from -28 to 28
- cache_keys: bfloat16 [256, 128, 1024], P(('grp', 'blk')), parts along dimension 0, may hold values from -24 to 24
- pool_values_prior: bfloat16 [256, 128, 1024], P(('grp', 'blk')), parts along dimension 0, may hold values from -6 to 6
- prefill_keys: bfloat16 [64, 128, 1024], P(('grp', 'blk')), parts along dimension 0, may hold values from -6 to 6
- prefill_values: bfloat16 [64, 128, 1024], P(('grp', 'blk')), parts along dimension 0, may hold values from -6 to 6
- context_lengths: int32 [16], P('grp'), parts along dimension 0, may hold values from 516 to 2048, as said below
- block_table: int32 [16, 16], P('grp'), parts along dimension 0, may hold values from 0 to 63, as said below
- spill_slots: int32 [64], P('grp'), parts along dimension 0, may hold values from 0 to 63, as said below
Outputs:
- attended: bfloat16 [64, 5120], P(('grp', 'blk')), parts along dimension 0
- pool_keys: bfloat16 [256, 128, 1024], P(('grp', 'blk')), parts along dimension 0
- pool_values: bfloat16 [256, 128, 1024], P(('grp', 'blk')), parts along dimension 0
There are 4 independent parts, one for each index of `grp`. A program takes and returns all parts, laid end to end along the dimension named above; each array names one. Nothing has to cross between parts.
Inputs may be any that keep to these rules, and one draw needn't show every extreme that they name: Every pool block appears exactly once in block_table, so each request owns 16 blocks. `spill_slots`: distinct pool blocks; exactly 2 of them lie in each rank's range of 8 blocks, and each stands among the first 4 columns of some row of block_table. `context_lengths`: some request has 2048 tokens.
All inputs are finite; a program needn't handle non-finite values.
Results may differ from a plain program's by a relative error of at most 0.0045.
Values may be sent and summed in bfloat16 or wider, within the bound.
A program may use at most 128 MiB of HBM per device.

v0:
```python
import jax
import jax.numpy as jnp
from jax import lax
from jax.sharding import PartitionSpec as P

QUERY_HEADS = 40
KEY_VALUE_HEADS = 8
HEAD_SIZE = 128
STEPS = 4
REQ = 4


NEGATIVE_LARGE = -1e30


def shifted(value, axis, steps):
    count = lax.axis_size(axis)
    pairs = [(source, (source + steps) % count) for source in range(count)]
    return lax.ppermute(value, axis, pairs)


def merge_state(running, incoming):
    run_max, run_sum, run_out = running
    new_max, new_sum, new_out = incoming
    largest = jnp.maximum(run_max, new_max)
    keep = jnp.exp(run_max - largest)
    take = jnp.exp(new_max - largest)
    return (
        largest,
        run_sum * keep + new_sum * take,
        run_out * keep[..., None] + new_out * take[..., None],
    )


def local_partial(decode_query_rows, first_row, owner, limit, keys_of_block, values_of_block):
    block_count, query_width = decode_query_rows.shape
    rank_slots, block_index, width = keys_of_block.shape
    head_groups = QUERY_HEADS // KEY_VALUE_HEADS
    row_ids = first_row + jnp.arange(block_count, dtype=jnp.int32)
    step_of = row_ids // REQ
    request_of = row_ids % REQ
    query_head_rows = decode_query_rows.reshape(
        block_count, KEY_VALUE_HEADS, head_groups, HEAD_SIZE
    )
    key_head_rows = keys_of_block.reshape(rank_slots, block_index, KEY_VALUE_HEADS, HEAD_SIZE)
    scores = jnp.einsum(
        "rhgd,sthd->rhgst", query_head_rows, key_head_rows, preferred_element_type=jnp.float32
    ) * HEAD_SIZE ** (-0.5)
    bound = limit[None, :] - (STEPS - 1) + step_of[:, None]
    visible = jnp.arange(block_index, dtype=jnp.int32)[None, None, :] < bound[:, :, None]
    visible = visible & (owner[None, :] == request_of[:, None])[:, :, None]
    visible = visible[:, None, None]
    masked = jnp.where(visible, scores, NEGATIVE_LARGE)
    row_max = jnp.max(masked, axis=(-2, -1))
    weights = jnp.where(visible, jnp.exp(masked - row_max[..., None, None]), 0.0)
    row_sum = jnp.sum(weights, axis=(-2, -1))
    probs = weights.astype(jnp.bfloat16)
    value_head_rows = values_of_block.reshape(rank_slots, block_index, KEY_VALUE_HEADS, HEAD_SIZE)
    row_out = jnp.einsum(
        "rhgst,sthd->rhgd", probs, value_head_rows, preferred_element_type=jnp.float32
    )
    return (row_max, row_sum, row_out)


def per_device(
    queries,
    cache_keys,
    pool_values_prior,
    prefill_keys,
    prefill_values,
    context_lengths,
    block_table,
    spill_slots,
):
    ranks = lax.axis_size("blk")
    myself = lax.axis_index("blk")
    rank_slots, block_index, width = cache_keys.shape
    per_rank = prefill_keys.shape[0]
    total_spill = spill_slots.shape[0]
    local_first = myself * rank_slots
    target_rank = spill_slots // rank_slots
    sequence = jnp.arange(total_spill, dtype=jnp.int32)
    mine = target_rank == myself
    landing_all = spill_slots - local_first
    placing_ids = jnp.arange(rank_slots, dtype=jnp.int32)
    source_rank = sequence // per_rank
    same_pair = (target_rank[None, :] == target_rank[:, None]) & (
        source_rank[None, :] == source_rank[:, None]
    )
    order = jnp.sum((same_pair & (sequence[None, :] < sequence[:, None])).astype(jnp.int32), axis=1)
    own_target = lax.dynamic_slice_in_dim(target_rank, myself * per_rank, per_rank, 0)
    own_order = lax.dynamic_slice_in_dim(order, myself * per_rank, per_rank, 0)
    peers = jnp.arange(ranks, dtype=jnp.int32)
    lanes = jnp.arange(per_rank, dtype=jnp.int32)
    sending = (peers[:, None, None] == own_target[None, None, :]) & (
        lanes[None, :, None] == own_order[None, None, :]
    )
    sending_bf = sending.astype(jnp.bfloat16)
    send_keys = jnp.einsum(
        "dqb,btw->dqtw", sending_bf, prefill_keys, preferred_element_type=jnp.float32
    ).astype(jnp.bfloat16)
    send_values = jnp.einsum(
        "dqb,btw->dqtw", sending_bf, prefill_values, preferred_element_type=jnp.float32
    ).astype(jnp.bfloat16)
    got_keys, got_values = (
        lax.all_to_all(send_keys, "blk", split_axis=0, concat_axis=0, tiled=True),
        lax.all_to_all(send_values, "blk", split_axis=0, concat_axis=0, tiled=True),
    )
    got_keys = got_keys.reshape(ranks * per_rank, block_index, width)
    got_values = got_values.reshape(ranks * per_rank, block_index, width)
    position = source_rank * per_rank + order
    columns = jnp.arange(ranks * per_rank, dtype=jnp.int32)
    hit = (
        mine[None, None, :]
        & (placing_ids[:, None, None] == landing_all[None, None, :])
        & (columns[None, :, None] == position[None, None, :])
    )
    placing = jnp.any(hit, axis=2)
    arrived_keys, arrived_values = (got_keys, got_values)
    filled = jnp.any(placing, axis=1)[:, None, None]
    placing_bf = placing.astype(jnp.bfloat16)
    placed_keys = jnp.einsum(
        "sk,ktw->stw", placing_bf, arrived_keys, preferred_element_type=jnp.float32
    ).astype(jnp.bfloat16)
    placed_values = jnp.einsum(
        "sk,ktw->stw", placing_bf, arrived_values, preferred_element_type=jnp.float32
    ).astype(jnp.bfloat16)
    pool_keys = jnp.where(filled, placed_keys, cache_keys)
    pool_values = jnp.where(filled, placed_values, pool_values_prior)
    local_ids = local_first + jnp.arange(rank_slots, dtype=jnp.int32)
    matches = block_table[:, :, None] == local_ids[None, None, :]
    request_ids = jnp.arange(block_table.shape[0], dtype=jnp.int32)[:, None, None]
    owner = jnp.sum(jnp.where(matches, request_ids, 0), axis=(0, 1))
    columns_t = jnp.arange(block_table.shape[1], dtype=jnp.int32)[None, :, None]
    limit = jnp.sum(
        jnp.where(matches, context_lengths[:, None, None] - columns_t * block_index, 0), axis=(0, 1)
    )
    rank_block_count, query_width = queries.shape
    head_groups = QUERY_HEADS // KEY_VALUE_HEADS
    starting = (
        jnp.full((rank_block_count, KEY_VALUE_HEADS, head_groups), NEGATIVE_LARGE, jnp.float32),
        jnp.zeros((rank_block_count, KEY_VALUE_HEADS, head_groups), jnp.float32),
        jnp.zeros((rank_block_count, KEY_VALUE_HEADS, head_groups, HEAD_SIZE), jnp.float32),
    )

    def advance(index, carried):
        visiting, running = carried
        anchor = (myself - index) % ranks
        running = merge_state(
            running,
            local_partial(
                visiting, anchor * rank_block_count, owner, limit, pool_keys, pool_values
            ),
        )
        visiting = shifted(visiting, "blk", 1)
        running = shifted((running[0], running[1], running[2]), "blk", 1)
        return (visiting, running)

    finished, running = lax.fori_loop(0, ranks, advance, (queries, starting))
    totals = running[1]
    outputs = running[2]
    attended = outputs / totals[..., None]
    attended = attended.reshape(rank_block_count, query_width).astype(jnp.bfloat16)
    return (attended, pool_keys, pool_values)


def solution(mesh):
    placed = (
        P(("grp", "blk"), None),
        P(("grp", "blk"), None, None),
        P(("grp", "blk"), None, None),
        P(("grp", "blk"), None, None),
        P(("grp", "blk"), None, None),
        P("grp"),
        P("grp", None),
        P("grp"),
    )
    return jax.shard_map(
        per_device,
        mesh=mesh,
        in_specs=placed,
        out_specs=(
            P(("grp", "blk"), None),
            P(("grp", "blk"), None, None),
            P(("grp", "blk"), None, None),
        ),
        check_vma=False,
    )
```

profile of v0, /device:TPU:0, one launch (start us, length us, event | category | flops | bytes accessed | tf_op | source)
XLA Modules:
  0.0 321.0 jit_solution(16954128831238491007)
XLA Ops:
  0.6 0.7 broadcast_compare_fusion.1
  1.7 2.6 convolution_convert_fusion.1
  4.3 4.3 %copy.83 = bf16[8,2,128,1024]{3,2,1,0:T(8,128)(2,1)} copy(bf16[8,2,128,1024]{3,0,2,1:T(8,128)(2,1)S(1)} %convolution_convert_fusion.1) | data formatting | bytes 8388608 | tf_op jit(solution)/shard_map/convert_element_type | solution.py:101
  8.6 6.5 %all-to-all-start = ((bf16[8,2,128,1024]{3,2,1,0:T(8,128)(2,1)}), bf16[8,2,128,1024]{3,2,1,0:T(8,128)(2,1)}, u32[]{:S(2)}, u32[]{:S(2)}) async-start(bf16[8,2,128,1024]{3,2,1,0:T(8,128)(2,1)} %copy.83), calls=%async_computation | async-start | bytes 8388608 | tf_op jit(solution)/shard_map/all_to_all | solution.py:106
  15.1 1.6 convolution_convert_fusion
  16.7 4.3 %copy.87 = bf16[8,2,128,1024]{3,2,1,0:T(8,128)(2,1)} copy(bf16[8,2,128,1024]{3,0,2,1:T(8,128)(2,1)S(1)} %convolution_convert_fusion) | data formatting | bytes 8388608 | tf_op jit(solution)/shard_map/convert_element_type | solution.py:104
  21.0 88.2 %all-to-all-done = bf16[8,2,128,1024]{3,2,1,0:T(8,128)(2,1)} async-done(((bf16[8,2,128,1024]{3,2,1,0:T(8,128)(2,1)}), bf16[8,2,128,1024]{3,2,1,0:T(8,128)(2,1)}, u32[]{:S(2)}, u32[]{:S(2)}) %all-to-all-start) | async-done | bytes 4194336 | tf_op jit(solution)/shard_map/all_to_all | solution.py:106
  109.2 4.8 %all-to-all-start.1 = ((bf16[8,2,128,1024]{3,2,1,0:T(8,128)(2,1)}), bf16[8,2,128,1024]{3,2,1,0:T(8,128)(2,1)}, u32[]{:S(2)}, u32[]{:S(2)}) async-start(bf16[8,2,128,1024]{3,2,1,0:T(8,128)(2,1)} %copy.87), calls=%async_computation.1 | async-start | bytes 8388608 | tf_op jit(solution)/shard_map/all_to_all | solution.py:107
  114.7 6.3 %copy_select_fusion.1 = bf16[8,128,1024]{2,0,1:T(8,128)(2,1)S(1)} fusion(bf16[8,128,1024]{2,1,0:T(8,128)(2,1)} %param.11, pred[8]{0:T(512)(128)(4,1)S(1)} %get-tuple-element.355, bf16[16,128,1024]{2,1,0:T(8,128)(2,1)} %bitcast.11, pred[8,16]{1,0:T(8,128)(4,1)S(1)} %get-tuple-element.354), kind=kOutput, calls=%fused_computation.38 | convolution fusion | flops 35651584 | bytes 8388744 | tf_op jit(solution)/shard_map/sk,ktw->stw/dot_general | solution.py:122
  121.1 1.2 copy.90
  122.2 85.6 %all-to-all-done.1 = bf16[8,2,128,1024]{3,2,1,0:T(8,128)(2,1)} async-done(((bf16[8,2,128,1024]{3,2,1,0:T(8,128)(2,1)}), bf16[8,2,128,1024]{3,2,1,0:T(8,128)(2,1)}, u32[]{:S(2)}, u32[]{:S(2)}) %all-to-all-start.1) | async-done | bytes 4194336 | tf_op jit(solution)/shard_map/all_to_all | solution.py:107
  207.8 6.3 %copy_select_fusion = bf16[8,128,1024]{2,0,1:T(8,128)(2,1)S(1)} fusion(bf16[8,128,1024]{2,1,0:T(8,128)(2,1)} %param.12, pred[8]{0:T(512)(128)(4,1)S(1)} %get-tuple-element.355, bf16[16,128,1024]{2,1,0:T(8,128)(2,1)} %bitcast.14, pred[8,16]{1,0:T(8,128)(4,1)S(1)} %get-tuple-element.354), kind=kOutput, calls=%fused_computation.37 | convolution fusion | flops 35651584 | bytes 8388744 | tf_op jit(solution)/shard_map/sk,ktw->stw/dot_general | solution.py:125
  214.2 2.5 copy.91
  216.6 103.0 %while.22 = (s32[]{:T(128)}, bf16[2,5120]{1,0:T(2,128)(2,1)S(1)}, f32[2,8,5]{2,1,0:T(8,128)S(1)}, f32[2,8,5]{2,1,0:T(8,128)S(1)}, f32[2,8,5,128]{3,2,0,1:T(8,128...) while((s32[]{:T(128)}, bf16[2,5120]{1,0:T(2,128)(2,1)S(1)}, ...), condition=%wide.region_8.9_spmd, body=%wide.region_5.8_spmd.sunk | while | flops 42715536 | bytes 31115856 | solution.py:159
  217.6 1.5 bitcast_bitcast_fusion.4
  219.3 2.4 fusion.61
  223.2 0.6 fusion.65
  224.2 5.5 %collective-permute-done.1 = f32[2,8,5]{2,1,0:T(8,128)S(1)} collective-permute-done((f32[2,8,5]{2,1,0:T(8,128)S(1)}, f32[2,8,5]{2,1,0:T(8,128)S(1)}, u32[]{:S(2)}, u32[]{:S(2)}) %collective-permute-start.1) | collective-permute-done | bytes 352 | tf_op jit(solution)/shard_map/while/body/eval_jaxpr/ppermute | solution.py:19
  230.4 1.5 bitcast_bitcast_fusion.4
  232.1 2.4 fusion.61
  236.0 0.6 fusion.65
  237.1 5.4 %collective-permute-done.1 = f32[2,8,5]{2,1,0:T(8,128)S(1)} collective-permute-done((f32[2,8,5]{2,1,0:T(8,128)S(1)}, f32[2,8,5]{2,1,0:T(8,128)S(1)}, u32[]{:S(2)}, u32[]{:S(2)}) %collective-permute-start.1) | collective-permute-done | bytes 352 | tf_op jit(solution)/shard_map/while/body/eval_jaxpr/ppermute | solution.py:19
  243.2 1.5 bitcast_bitcast_fusion.4
  245.0 2.4 fusion.61
  248.9 0.6 fusion.65
  249.9 5.4 %collective-permute-done.1 = f32[2,8,5]{2,1,0:T(8,128)S(1)} collective-permute-done((f32[2,8,5]{2,1,0:T(8,128)S(1)}, f32[2,8,5]{2,1,0:T(8,128)S(1)}, u32[]{:S(2)}, u32[]{:S(2)}) %collective-permute-start.1) | collective-permute-done | bytes 352 | tf_op jit(solution)/shard_map/while/body/eval_jaxpr/ppermute | solution.py:19
  256.1 1.5 bitcast_bitcast_fusion.4
  257.8 2.4 fusion.61
  261.7 0.6 fusion.65
  262.8 5.4 %collective-permute-done.1 = f32[2,8,5]{2,1,0:T(8,128)S(1)} collective-permute-done((f32[2,8,5]{2,1,0:T(8,128)S(1)}, f32[2,8,5]{2,1,0:T(8,128)S(1)}, u32[]{:S(2)}, u32[]{:S(2)}) %collective-permute-start.1) | collective-permute-done | bytes 352 | tf_op jit(solution)/shard_map/while/body/eval_jaxpr/ppermute | solution.py:19
  268.9 1.5 bitcast_bitcast_fusion.4
  270.7 2.4 fusion.61
  273.8 0.6 copy.167
  274.6 0.6 fusion.65
  275.6 5.4 %collective-permute-done.1 = f32[2,8,5]{2,1,0:T(8,128)S(1)} collective-permute-done((f32[2,8,5]{2,1,0:T(8,128)S(1)}, f32[2,8,5]{2,1,0:T(8,128)S(1)}, u32[]{:S(2)}, u32[]{:S(2)}) %collective-permute-start.1) | collective-permute-done | bytes 352 | tf_op jit(solution)/shard_map/while/body/eval_jaxpr/ppermute | solution.py:19
  281.8 1.5 bitcast_bitcast_fusion.4
  283.5 2.4 fusion.61
  287.4 0.6 fusion.65
  288.5 5.4 %collective-permute-done.1 = f32[2,8,5]{2,1,0:T(8,128)S(1)} collective-permute-done((f32[2,8,5]{2,1,0:T(8,128)S(1)}, f32[2,8,5]{2,1,0:T(8,128)S(1)}, u32[]{:S(2)}, u32[]{:S(2)}) %collective-permute-start.1) | collective-permute-done | bytes 352 | tf_op jit(solution)/shard_map/while/body/eval_jaxpr/ppermute | solution.py:19
  294.6 1.5 bitcast_bitcast_fusion.4
  296.4 2.4 fusion.61
  300.2 0.6 fusion.65
  301.3 5.4 %collective-permute-done.1 = f32[2,8,5]{2,1,0:T(8,128)S(1)} collective-permute-done((f32[2,8,5]{2,1,0:T(8,128)S(1)}, f32[2,8,5]{2,1,0:T(8,128)S(1)}, u32[]{:S(2)}, u32[]{:S(2)}) %collective-permute-start.1) | collective-permute-done | bytes 352 | tf_op jit(solution)/shard_map/while/body/eval_jaxpr/ppermute | solution.py:19
  307.5 1.5 bitcast_bitcast_fusion.4
  309.2 2.4 fusion.61
  313.1 0.6 fusion.65
  314.1 5.4 %collective-permute-done.1 = f32[2,8,5]{2,1,0:T(8,128)S(1)} collective-permute-done((f32[2,8,5]{2,1,0:T(8,128)S(1)}, f32[2,8,5]{2,1,0:T(8,128)S(1)}, u32[]{:S(2)}, u32[]{:S(2)}) %collective-permute-start.1) | collective-permute-done | bytes 352 | tf_op jit(solution)/shard_map/while/body/eval_jaxpr/ppermute | solution.py:19
  319.8 0.8 convert_element_type.40
  (224 shorter events, 23.3 us)
Async XLA Ops:
  8.6 6.5 %copy-start.3 = (bf16[2,128,1024]{2,1,0:T(8,128)(2,1)S(1)}, bf16[2,128,1024]{2,1,0:T(8,128)(2,1)}, u32[]{:S(2)}) copy-start(bf16[2,128,1024]{2,1,0:T(8,128)(2,1)} %param.14) | copy-start | bytes 1572868
  8.6 100.6 %all-to-all-start = ((bf16[8,2,128,1024]{3,2,1,0:T(8,128)(2,1)}), bf16[8,2,128,1024]{3,2,1,0:T(8,128)(2,1)}, u32[]{:S(2)}, u32[]{:S(2)}) async-start(bf16[8,2,128,1024]{3,2,1,0:T(8,128)(2,1)} %copy.83), calls=%async_computation | async-start | bytes 8388608 | tf_op jit(solution)/shard_map/all_to_all | solution.py:106
  21.0 93.0 %copy-start.5 = (s32[16]{0:T(128)S(1)}, s32[16]{0:T(128)}, u32[]{:S(2)}) copy-start(s32[16]{0:T(128)} %param.17) | copy-start | bytes 196
  21.0 93.4 %copy-start.6 = (s32[4]{0:T(128)S(1)}, s32[4]{0:T(128)}, u32[]{:S(2)}) copy-start(s32[4]{0:T(128)} %param.15) | copy-start | bytes 52
  21.0 93.5 %copy-start.4 = (s32[4,16]{1,0:T(4,128)S(1)}, s32[4,16]{1,0:T(4,128)}, u32[]{:S(2)}) copy-start(s32[4,16]{1,0:T(4,128)} %param.16) | copy-start | bytes 772
  109.2 98.6 %all-to-all-start.1 = ((bf16[8,2,128,1024]{3,2,1,0:T(8,128)(2,1)}), bf16[8,2,128,1024]{3,2,1,0:T(8,128)(2,1)}, u32[]{:S(2)}, u32[]{:S(2)}) async-start(bf16[8,2,128,1024]{3,2,1,0:T(8,128)(2,1)} %copy.87), calls=%async_computation.1 | async-start | bytes 8388608 | tf_op jit(solution)/shard_map/all_to_all | solution.py:107
  214.1 2.5 copy-start.2
  219.3 3.1 copy-start.1
  223.8 5.9 %collective-permute-start.3 = (f32[2,8,5,128]{3,2,0,1:T(8,128)S(1)}, f32[2,8,5,128]{3,2,0,1:T(8,128)S(1)}, u32[]{:S(2)}, u32[]{:S(2)}) collective-permute-start(f32[2,8,5,128]{3,2,0,1:T(8,128)S(1)} %fusion.65), channel_id=1, source_target_pairs={{0,4},{4,8},{8,12},{12,16},{16,20},{20,24},{24,28},{28,0},{1,5},{5... | collective-permute-start | bytes 122888 | tf_op jit(solution)/shard_map/while/body/eval_jaxpr/ppermute | solution.py:19
  223.9 5.9 %collective-permute-start = (bf16[2,5120]{1,0:T(2,128)(2,1)S(1)}, bf16[2,5120]{1,0:T(2,128)(2,1)S(1)}, u32[]{:S(2)}, u32[]{:S(2)}) collective-permute-start(bf16[2,5120]{1,0:T(2,128)(2,1)S(1)} %copy.176), channel_id=1, source_target_pairs={{0,4},{4,8},{8,12},{12,16},{16,20},{20,24},{24,28},{28,0},{1,5},{5... | collective-permute-start | bytes 61448 | tf_op jit(solution)/shard_map/while/body/eval_jaxpr/ppermute | solution.py:19
  223.9 5.7 %collective-permute-start.1 = (f32[2,8,5]{2,1,0:T(8,128)S(1)}, f32[2,8,5]{2,1,0:T(8,128)S(1)}, u32[]{:S(2)}, u32[]{:S(2)}) collective-permute-start(f32[2,8,5]{2,1,0:T(8,128)S(1)} %get-tuple-element.460), channel_id=1, source_target_pairs={{0,4},{4,8},{8,12},{12,16},{16,20},{20,24},{24,28},{28,0},{1,5},{5... | collective-permute-start | bytes 968 | tf_op jit(solution)/shard_map/while/body/eval_jaxpr/ppermute | solution.py:19
  224.0 5.7 %collective-permute-start.2 = (f32[2,8,5]{2,1,0:T(8,128)S(1)}, f32[2,8,5]{2,1,0:T(8,128)S(1)}, u32[]{:S(2)}, u32[]{:S(2)}) collective-permute-start(f32[2,8,5]{2,1,0:T(8,128)S(1)} %get-tuple-element.461), channel_id=1, source_target_pairs={{0,4},{4,8},{8,12},{12,16},{16,20},{20,24},{24,28},{28,0},{1,5},{5... | collective-permute-start | bytes 968 | tf_op jit(solution)/shard_map/while/body/eval_jaxpr/ppermute | solution.py:19
  232.1 3.1 copy-start.1
  236.7 5.9 %collective-permute-start.3 = (f32[2,8,5,128]{3,2,0,1:T(8,128)S(1)}, f32[2,8,5,128]{3,2,0,1:T(8,128)S(1)}, u32[]{:S(2)}, u32[]{:S(2)}) collective-permute-start(f32[2,8,5,128]{3,2,0,1:T(8,128)S(1)} %fusion.65), channel_id=1, source_target_pairs={{0,4},{4,8},{8,12},{12,16},{16,20},{20,24},{24,28},{28,0},{1,5},{5... | collective-permute-start | bytes 122888 | tf_op jit(solution)/shard_map/while/body/eval_jaxpr/ppermute | solution.py:19
  236.7 5.9 %collective-permute-start = (bf16[2,5120]{1,0:T(2,128)(2,1)S(1)}, bf16[2,5120]{1,0:T(2,128)(2,1)S(1)}, u32[]{:S(2)}, u32[]{:S(2)}) collective-permute-start(bf16[2,5120]{1,0:T(2,128)(2,1)S(1)} %copy.176), channel_id=1, source_target_pairs={{0,4},{4,8},{8,12},{12,16},{16,20},{20,24},{24,28},{28,0},{1,5},{5... | collective-permute-start | bytes 61448 | tf_op jit(solution)/shard_map/while/body/eval_jaxpr/ppermute | solution.py:19
  236.8 5.7 %collective-permute-start.1 = (f32[2,8,5]{2,1,0:T(8,128)S(1)}, f32[2,8,5]{2,1,0:T(8,128)S(1)}, u32[]{:S(2)}, u32[]{:S(2)}) collective-permute-start(f32[2,8,5]{2,1,0:T(8,128)S(1)} %get-tuple-element.460), channel_id=1, source_target_pairs={{0,4},{4,8},{8,12},{12,16},{16,20},{20,24},{24,28},{28,0},{1,5},{5... | collective-permute-start | bytes 968 | tf_op jit(solution)/shard_map/while/body/eval_jaxpr/ppermute | solution.py:19
  236.9 5.7 %collective-permute-start.2 = (f32[2,8,5]{2,1,0:T(8,128)S(1)}, f32[2,8,5]{2,1,0:T(8,128)S(1)}, u32[]{:S(2)}, u32[]{:S(2)}) collective-permute-start(f32[2,8,5]{2,1,0:T(8,128)S(1)} %get-tuple-element.461), channel_id=1, source_target_pairs={{0,4},{4,8},{8,12},{12,16},{16,20},{20,24},{24,28},{28,0},{1,5},{5... | collective-permute-start | bytes 968 | tf_op jit(solution)/shard_map/while/body/eval_jaxpr/ppermute | solution.py:19
  245.0 3.1 copy-start.1
  249.5 5.9 %collective-permute-start.3 = (f32[2,8,5,128]{3,2,0,1:T(8,128)S(1)}, f32[2,8,5,128]{3,2,0,1:T(8,128)S(1)}, u32[]{:S(2)}, u32[]{:S(2)}) collective-permute-start(f32[2,8,5,128]{3,2,0,1:T(8,128)S(1)} %fusion.65), channel_id=1, source_target_pairs={{0,4},{4,8},{8,12},{12,16},{16,20},{20,24},{24,28},{28,0},{1,5},{5... | collective-permute-start | bytes 122888 | tf_op jit(solution)/shard_map/while/body/eval_jaxpr/ppermute | solution.py:19
  249.6 5.9 %collective-permute-start = (bf16[2,5120]{1,0:T(2,128)(2,1)S(1)}, bf16[2,5120]{1,0:T(2,128)(2,1)S(1)}, u32[]{:S(2)}, u32[]{:S(2)}) collective-permute-start(bf16[2,5120]{1,0:T(2,128)(2,1)S(1)} %copy.176), channel_id=1, source_target_pairs={{0,4},{4,8},{8,12},{12,16},{16,20},{20,24},{24,28},{28,0},{1,5},{5... | collective-permute-start | bytes 61448 | tf_op jit(solution)/shard_map/while/body/eval_jaxpr/ppermute | solution.py:19
  249.6 5.7 %collective-permute-start.1 = (f32[2,8,5]{2,1,0:T(8,128)S(1)}, f32[2,8,5]{2,1,0:T(8,128)S(1)}, u32[]{:S(2)}, u32[]{:S(2)}) collective-permute-start(f32[2,8,5]{2,1,0:T(8,128)S(1)} %get-tuple-element.460), channel_id=1, source_target_pairs={{0,4},{4,8},{8,12},{12,16},{16,20},{20,24},{24,28},{28,0},{1,5},{5... | collective-permute-start | bytes 968 | tf_op jit(solution)/shard_map/while/body/eval_jaxpr/ppermute | solution.py:19
  249.7 5.7 %collective-permute-start.2 = (f32[2,8,5]{2,1,0:T(8,128)S(1)}, f32[2,8,5]{2,1,0:T(8,128)S(1)}, u32[]{:S(2)}, u32[]{:S(2)}) collective-permute-start(f32[2,8,5]{2,1,0:T(8,128)S(1)} %get-tuple-element.461), channel_id=1, source_target_pairs={{0,4},{4,8},{8,12},{12,16},{16,20},{20,24},{24,28},{28,0},{1,5},{5... | collective-permute-start | bytes 968 | tf_op jit(solution)/shard_map/while/body/eval_jaxpr/ppermute | solution.py:19
  257.8 3.1 copy-start.1
  262.4 5.9 %collective-permute-start.3 = (f32[2,8,5,128]{3,2,0,1:T(8,128)S(1)}, f32[2,8,5,128]{3,2,0,1:T(8,128)S(1)}, u32[]{:S(2)}, u32[]{:S(2)}) collective-permute-start(f32[2,8,5,128]{3,2,0,1:T(8,128)S(1)} %fusion.65), channel_id=1, source_target_pairs={{0,4},{4,8},{8,12},{12,16},{16,20},{20,24},{24,28},{28,0},{1,5},{5... | collective-permute-start | bytes 122888 | tf_op jit(solution)/shard_map/while/body/eval_jaxpr/ppermute | solution.py:19
  262.4 5.9 %collective-permute-start = (bf16[2,5120]{1,0:T(2,128)(2,1)S(1)}, bf16[2,5120]{1,0:T(2,128)(2,1)S(1)}, u32[]{:S(2)}, u32[]{:S(2)}) collective-permute-start(bf16[2,5120]{1,0:T(2,128)(2,1)S(1)} %copy.176), channel_id=1, source_target_pairs={{0,4},{4,8},{8,12},{12,16},{16,20},{20,24},{24,28},{28,0},{1,5},{5... | collective-permute-start | bytes 61448 | tf_op jit(solution)/shard_map/while/body/eval_jaxpr/ppermute | solution.py:19
  262.5 5.7 %collective-permute-start.1 = (f32[2,8,5]{2,1,0:T(8,128)S(1)}, f32[2,8,5]{2,1,0:T(8,128)S(1)}, u32[]{:S(2)}, u32[]{:S(2)}) collective-permute-start(f32[2,8,5]{2,1,0:T(8,128)S(1)} %get-tuple-element.460), channel_id=1, source_target_pairs={{0,4},{4,8},{8,12},{12,16},{16,20},{20,24},{24,28},{28,0},{1,5},{5... | collective-permute-start | bytes 968 | tf_op jit(solution)/shard_map/while/body/eval_jaxpr/ppermute | solution.py:19
  262.5 5.7 %collective-permute-start.2 = (f32[2,8,5]{2,1,0:T(8,128)S(1)}, f32[2,8,5]{2,1,0:T(8,128)S(1)}, u32[]{:S(2)}, u32[]{:S(2)}) collective-permute-start(f32[2,8,5]{2,1,0:T(8,128)S(1)} %get-tuple-element.461), channel_id=1, source_target_pairs={{0,4},{4,8},{8,12},{12,16},{16,20},{20,24},{24,28},{28,0},{1,5},{5... | collective-permute-start | bytes 968 | tf_op jit(solution)/shard_map/while/body/eval_jaxpr/ppermute | solution.py:19
  270.7 3.1 copy-start.1
  275.2 5.9 %collective-permute-start.3 = (f32[2,8,5,128]{3,2,0,1:T(8,128)S(1)}, f32[2,8,5,128]{3,2,0,1:T(8,128)S(1)}, u32[]{:S(2)}, u32[]{:S(2)}) collective-permute-start(f32[2,8,5,128]{3,2,0,1:T(8,128)S(1)} %fusion.65), channel_id=1, source_target_pairs={{0,4},{4,8},{8,12},{12,16},{16,20},{20,24},{24,28},{28,0},{1,5},{5... | collective-permute-start | bytes 122888 | tf_op jit(solution)/shard_map/while/body/eval_jaxpr/ppermute | solution.py:19
  275.3 5.9 %collective-permute-start = (bf16[2,5120]{1,0:T(2,128)(2,1)S(1)}, bf16[2,5120]{1,0:T(2,128)(2,1)S(1)}, u32[]{:S(2)}, u32[]{:S(2)}) collective-permute-start(bf16[2,5120]{1,0:T(2,128)(2,1)S(1)} %copy.176), channel_id=1, source_target_pairs={{0,4},{4,8},{8,12},{12,16},{16,20},{20,24},{24,28},{28,0},{1,5},{5... | collective-permute-start | bytes 61448 | tf_op jit(solution)/shard_map/while/body/eval_jaxpr/ppermute | solution.py:19
  275.3 5.7 %collective-permute-start.1 = (f32[2,8,5]{2,1,0:T(8,128)S(1)}, f32[2,8,5]{2,1,0:T(8,128)S(1)}, u32[]{:S(2)}, u32[]{:S(2)}) collective-permute-start(f32[2,8,5]{2,1,0:T(8,128)S(1)} %get-tuple-element.460), channel_id=1, source_target_pairs={{0,4},{4,8},{8,12},{12,16},{16,20},{20,24},{24,28},{28,0},{1,5},{5... | collective-permute-start | bytes 968 | tf_op jit(solution)/shard_map/while/body/eval_jaxpr/ppermute | solution.py:19
  275.4 5.7 %collective-permute-start.2 = (f32[2,8,5]{2,1,0:T(8,128)S(1)}, f32[2,8,5]{2,1,0:T(8,128)S(1)}, u32[]{:S(2)}, u32[]{:S(2)}) collective-permute-start(f32[2,8,5]{2,1,0:T(8,128)S(1)} %get-tuple-element.461), channel_id=1, source_target_pairs={{0,4},{4,8},{8,12},{12,16},{16,20},{20,24},{24,28},{28,0},{1,5},{5... | collective-permute-start | bytes 968 | tf_op jit(solution)/shard_map/while/body/eval_jaxpr/ppermute | solution.py:19
  283.5 3.1 copy-start.1
  288.0 5.9 %collective-permute-start.3 = (f32[2,8,5,128]{3,2,0,1:T(8,128)S(1)}, f32[2,8,5,128]{3,2,0,1:T(8,128)S(1)}, u32[]{:S(2)}, u32[]{:S(2)}) collective-permute-start(f32[2,8,5,128]{3,2,0,1:T(8,128)S(1)} %fusion.65), channel_id=1, source_target_pairs={{0,4},{4,8},{8,12},{12,16},{16,20},{20,24},{24,28},{28,0},{1,5},{5... | collective-permute-start | bytes 122888 | tf_op jit(solution)/shard_map/while/body/eval_jaxpr/ppermute | solution.py:19
  288.1 5.9 %collective-permute-start = (bf16[2,5120]{1,0:T(2,128)(2,1)S(1)}, bf16[2,5120]{1,0:T(2,128)(2,1)S(1)}, u32[]{:S(2)}, u32[]{:S(2)}) collective-permute-start(bf16[2,5120]{1,0:T(2,128)(2,1)S(1)} %copy.176), channel_id=1, source_target_pairs={{0,4},{4,8},{8,12},{12,16},{16,20},{20,24},{24,28},{28,0},{1,5},{5... | collective-permute-start | bytes 61448 | tf_op jit(solution)/shard_map/while/body/eval_jaxpr/ppermute | solution.py:19
  288.2 5.7 %collective-permute-start.1 = (f32[2,8,5]{2,1,0:T(8,128)S(1)}, f32[2,8,5]{2,1,0:T(8,128)S(1)}, u32[]{:S(2)}, u32[]{:S(2)}) collective-permute-start(f32[2,8,5]{2,1,0:T(8,128)S(1)} %get-tuple-element.460), channel_id=1, source_target_pairs={{0,4},{4,8},{8,12},{12,16},{16,20},{20,24},{24,28},{28,0},{1,5},{5... | collective-permute-start | bytes 968 | tf_op jit(solution)/shard_map/while/body/eval_jaxpr/ppermute | solution.py:19
  288.2 5.7 %collective-permute-start.2 = (f32[2,8,5]{2,1,0:T(8,128)S(1)}, f32[2,8,5]{2,1,0:T(8,128)S(1)}, u32[]{:S(2)}, u32[]{:S(2)}) collective-permute-start(f32[2,8,5]{2,1,0:T(8,128)S(1)} %get-tuple-element.461), channel_id=1, source_target_pairs={{0,4},{4,8},{8,12},{12,16},{16,20},{20,24},{24,28},{28,0},{1,5},{5... | collective-permute-start | bytes 968 | tf_op jit(solution)/shard_map/while/body/eval_jaxpr/ppermute | solution.py:19
  296.4 3.1 copy-start.1
  300.9 5.9 %collective-permute-start.3 = (f32[2,8,5,128]{3,2,0,1:T(8,128)S(1)}, f32[2,8,5,128]{3,2,0,1:T(8,128)S(1)}, u32[]{:S(2)}, u32[]{:S(2)}) collective-permute-start(f32[2,8,5,128]{3,2,0,1:T(8,128)S(1)} %fusion.65), channel_id=1, source_target_pairs={{0,4},{4,8},{8,12},{12,16},{16,20},{20,24},{24,28},{28,0},{1,5},{5... | collective-permute-start | bytes 122888 | tf_op jit(solution)/shard_map/while/body/eval_jaxpr/ppermute | solution.py:19
  301.0 5.9 %collective-permute-start = (bf16[2,5120]{1,0:T(2,128)(2,1)S(1)}, bf16[2,5120]{1,0:T(2,128)(2,1)S(1)}, u32[]{:S(2)}, u32[]{:S(2)}) collective-permute-start(bf16[2,5120]{1,0:T(2,128)(2,1)S(1)} %copy.176), channel_id=1, source_target_pairs={{0,4},{4,8},{8,12},{12,16},{16,20},{20,24},{24,28},{28,0},{1,5},{5... | collective-permute-start | bytes 61448 | tf_op jit(solution)/shard_map/while/body/eval_jaxpr/ppermute | solution.py:19
  301.0 5.7 %collective-permute-start.1 = (f32[2,8,5]{2,1,0:T(8,128)S(1)}, f32[2,8,5]{2,1,0:T(8,128)S(1)}, u32[]{:S(2)}, u32[]{:S(2)}) collective-permute-start(f32[2,8,5]{2,1,0:T(8,128)S(1)} %get-tuple-element.460), channel_id=1, source_target_pairs={{0,4},{4,8},{8,12},{12,16},{16,20},{20,24},{24,28},{28,0},{1,5},{5... | collective-permute-start | bytes 968 | tf_op jit(solution)/shard_map/while/body/eval_jaxpr/ppermute | solution.py:19
  301.1 5.7 %collective-permute-start.2 = (f32[2,8,5]{2,1,0:T(8,128)S(1)}, f32[2,8,5]{2,1,0:T(8,128)S(1)}, u32[]{:S(2)}, u32[]{:S(2)}) collective-permute-start(f32[2,8,5]{2,1,0:T(8,128)S(1)} %get-tuple-element.461), channel_id=1, source_target_pairs={{0,4},{4,8},{8,12},{12,16},{16,20},{20,24},{24,28},{28,0},{1,5},{5... | collective-permute-start | bytes 968 | tf_op jit(solution)/shard_map/while/body/eval_jaxpr/ppermute | solution.py:19
  309.2 3.1 copy-start.1
  313.7 5.9 %collective-permute-start.3 = (f32[2,8,5,128]{3,2,0,1:T(8,128)S(1)}, f32[2,8,5,128]{3,2,0,1:T(8,128)S(1)}, u32[]{:S(2)}, u32[]{:S(2)}) collective-permute-start(f32[2,8,5,128]{3,2,0,1:T(8,128)S(1)} %fusion.65), channel_id=1, source_target_pairs={{0,4},{4,8},{8,12},{12,16},{16,20},{20,24},{24,28},{28,0},{1,5},{5... | collective-permute-start | bytes 122888 | tf_op jit(solution)/shard_map/while/body/eval_jaxpr/ppermute | solution.py:19
  313.8 5.9 %collective-permute-start = (bf16[2,5120]{1,0:T(2,128)(2,1)S(1)}, bf16[2,5120]{1,0:T(2,128)(2,1)S(1)}, u32[]{:S(2)}, u32[]{:S(2)}) collective-permute-start(bf16[2,5120]{1,0:T(2,128)(2,1)S(1)} %copy.176), channel_id=1, source_target_pairs={{0,4},{4,8},{8,12},{12,16},{16,20},{20,24},{24,28},{28,0},{1,5},{5... | collective-permute-start | bytes 61448 | tf_op jit(solution)/shard_map/while/body/eval_jaxpr/ppermute | solution.py:19
  313.9 5.7 %collective-permute-start.1 = (f32[2,8,5]{2,1,0:T(8,128)S(1)}, f32[2,8,5]{2,1,0:T(8,128)S(1)}, u32[]{:S(2)}, u32[]{:S(2)}) collective-permute-start(f32[2,8,5]{2,1,0:T(8,128)S(1)} %get-tuple-element.460), channel_id=1, source_target_pairs={{0,4},{4,8},{8,12},{12,16},{16,20},{20,24},{24,28},{28,0},{1,5},{5... | collective-permute-start | bytes 968 | tf_op jit(solution)/shard_map/while/body/eval_jaxpr/ppermute | solution.py:19
  313.9 5.7 %collective-permute-start.2 = (f32[2,8,5]{2,1,0:T(8,128)S(1)}, f32[2,8,5]{2,1,0:T(8,128)S(1)}, u32[]{:S(2)}, u32[]{:S(2)}) collective-permute-start(f32[2,8,5]{2,1,0:T(8,128)S(1)} %get-tuple-element.461), channel_id=1, source_target_pairs={{0,4},{4,8},{8,12},{12,16},{16,20},{20,24},{24,28},{28,0},{1,5},{5... | collective-permute-start | bytes 968 | tf_op jit(solution)/shard_map/while/body/eval_jaxpr/ppermute | solution.py:19
  319.7 1.3 copy-start
where the time goes:
time: 321 us
  waiting for transfers between devices  218 us (68%)
  matrix products  41.3 us (13%)
  local copies, waits for them, and re-layouts  36.8 us (11%)
  starting transfers between devices  14.3 us (4%)
  other arithmetic  8.69 us (3%)
    all_to_all x1, waiting for transfers between devices, per_device(): lax.all_to_all(send_keys, 'blk', split_axis=0, concat_axis=0, tiled=True)  88.2 us
    all_to_all x1, waiting for transfers between devices, per_device(): lax.all_to_all(send_values, 'blk', split_axis=0, concat_axis=0, tiled=True)  85.6 us
    ppermute x32, waiting for transfers between devices, shifted(): return lax.ppermute(value, axis, pairs)  44.2 us
    dot_general x8, matrix products, local_partial(): jnp.einsum('rhgd,sthd->rhgst', query_head_rows, key_head_rows, preferred_...  19.2 us
    reshape x8, local copies, waits for them, and re-layouts, local_partial(): keys_of_block.reshape(rank_slots, block_index, KEY_VALUE_HEADS, HEAD_SIZE)  11.7 us
    while x32, local copies, waits for them, and re-layouts  9.97 us
    all_to_all x1, starting transfers between devices, per_device(): lax.all_to_all(send_keys, 'blk', split_axis=0, concat_axis=0, tiled=True)  6.46 us
  transfers between devices with their start and end apart: 34, of which 18 were waited for; matrix products, arithmetic and copies ran while one was open for 4% of the time, Pallas kernels for 0%

commit v1 on v0

v1 whole, which is shorter than its diff:
```python
import functools

import jax
import jax.numpy as jnp
from jax import lax
from jax.experimental import pallas as pl
from jax.experimental.pallas import tpu as pltpu
from jax.sharding import PartitionSpec as P

QUERY_HEADS = 40
KV = 8
GROUPS = QUERY_HEADS // KV
HEAD = 128
STEPS = 4
REQ = 4
ROWS = 16
PIECES = 4
HEADS_PER_STEP = 2
LOW = -1e30
FAR = 1 << 24
MESH = pl.DeviceIdType.MESH


def lane_plan(spill, chips, z, lanes, chip_blocks, rank_slots):
    total = chips * chip_blocks
    rank_of = [spill[b] // rank_slots for b in range(total)]
    chip_of = [r // 2 for r in rank_of]
    sends, arrivals = [], []
    for way in range(2):
        dest = chip_of if way == 0 else [chips - 1 - c for c in chip_of]
        place = z if way == 0 else chips - 1 - z
        lane_dest = [jnp.int32(-1)] * lanes
        lane_block = [jnp.int32(-1)] * lanes
        send = [jnp.int32(chip_blocks)] * lanes
        arrive = [jnp.int32(-1)] * lanes
        for n in range(chips):
            here = place == n
            if n > 0:
                arrive = [jnp.where(here, lane_block[l], arrive[l]) for l in range(lanes)]
            if n == chips - 1:
                break
            first = (n if way == 0 else chips - 1 - n) * chip_blocks
            left = [dest[first + i] > n for i in range(chip_blocks)]
            for l in reversed(range(min(lanes, chip_blocks * (n + 1)))):
                pick, pick_dest = jnp.int32(chip_blocks), jnp.int32(-1)
                for i in reversed(range(chip_blocks)):
                    pick = jnp.where(left[i], i, pick)
                    pick_dest = jnp.where(left[i], dest[first + i], pick_dest)
                take = (lane_dest[l] <= n) & (pick < chip_blocks)
                left = [left[i] & jnp.logical_not(take & (pick == i)) for i in range(chip_blocks)]
                lane_dest[l] = jnp.where(take, pick_dest, lane_dest[l])
                lane_block[l] = jnp.where(take, first + pick, lane_block[l])
                send[l] = jnp.where(here & take, pick, send[l])
        sends.append(send)
        arrivals.append(arrive)
    return rank_of, sends, arrivals


def blocks_for(rank, rank_of, per_rank):
    found = [jnp.int32(0)] * per_rank
    count = jnp.int32(0)
    for b, target in enumerate(rank_of):
        hit = target == rank
        found = [jnp.where(hit & (count == q), b, found[q]) for q in range(per_rank)]
        count = count + hit.astype(jnp.int32)
    return found


def exchange_kernel(
    chips, lanes, limits, spill, q_ref, pk, pv, ck, cv,
    att, newk, newv,
    kall, vall, own, arr, snd, fin, pout, pin, qg, bias, part, lse, pin_o, pin_l, mo, ml, ro, rl, sched,
    loc, ex_s, ex_r, q_s, q_r, lane_s, lane_r, s1_s, s1_r, s2_s, s2_r, fx_s, fx_r, out_s,
):
    rank_slots, tokens, width = ck.shape
    per_rank = pk.shape[0]
    chip_blocks = 2 * per_rank
    blocks = rank_slots + per_rank
    rows_here = STEPS * REQ // (2 * chips)
    piece = tokens // PIECES
    me = lax.axis_index("blk")
    z = me // 2
    core = lax.rem(me, 2)
    partner = 2 * z + 1 - core

    def remote(src, dst, s, r, rank):
        return pltpu.make_async_remote_copy(
            src_ref=src, dst_ref=dst, send_sem=s, recv_sem=r, device_id={"blk": rank}, device_id_type=MESH
        )

    load_kp = pltpu.make_async_copy(pk, kall.at[pl.ds(rank_slots, per_rank)], loc.at[0])
    load_vp = pltpu.make_async_copy(pv, vall.at[pl.ds(rank_slots, per_rank)], loc.at[1])
    load_kc = pltpu.make_async_copy(ck, kall.at[pl.ds(0, rank_slots)], loc.at[2])
    load_vc = pltpu.make_async_copy(cv, vall.at[pl.ds(0, rank_slots)], loc.at[3])
    own_mine = own.at[pl.ds(core * per_rank, per_rank)]

    @pl.when(core == 0)
    def _():
        pltpu.make_async_copy(pk, own_mine, loc.at[4]).start()

    @pl.when(core == 1)
    def _():
        pltpu.make_async_copy(pv, own_mine, loc.at[4]).start()

    load_kp.start()
    load_vp.start()
    load_kc.start()
    load_vc.start()

    barrier = pltpu.get_barrier_semaphore()
    pl.semaphore_signal(barrier, inc=1, device_id={"blk": partner}, device_id_type=MESH)
    for off in range(1, chips):
        peer = 2 * lax.rem(z + off, chips) + core
        pl.semaphore_signal(barrier, inc=1, device_id={"blk": peer}, device_id_type=MESH)
    pl.semaphore_wait(barrier, chips)

    @pl.when(core == 0)
    def _():
        remote(pv, own_mine, ex_s, ex_r, partner).start()

    @pl.when(core == 1)
    def _():
        remote(pk, own_mine, ex_s, ex_r, partner).start()

    mine = core * chips + z
    q_copies = [remote(q_ref, qg.at[mine], q_s.at[0], q_r.at[mine], partner)]
    for off in range(1, chips):
        peer = 2 * lax.rem(z + off, chips) + core
        q_copies.append(remote(q_ref, qg.at[mine], q_s.at[off], q_r.at[mine], peer))
    for copy in q_copies:
        copy.start()
    qg[mine] = q_ref[...]

    rank_of, sends, arrivals = lane_plan(spill, chips, z, lanes, chip_blocks, rank_slots)
    for way in range(2):
        for l in range(lanes):
            sched[way, l] = sends[way][l]

    pltpu.make_async_copy(pk, own_mine, loc.at[4]).wait()
    own_other = own.at[pl.ds((1 - core) * per_rank, per_rank)]
    arrived = remote(pk, own_other, ex_s, ex_r, partner)
    arrived.wait_recv()

    low_half = z < chips // 2
    near = jnp.where(low_half, z, chips - 1 - z)
    far = chips - 1 - near
    near_way = jnp.where(low_half, 0, 1)
    far_way = 1 - near_way
    near_next = 2 * jnp.where(low_half, z + 1, z - 1) + core
    far_next = 2 * jnp.where(low_half, jnp.maximum(z - 1, 0), jnp.minimum(z + 1, chips - 1)) + core

    def lane_copy(way, l, p, rank):
        rows = pl.ds(p * piece, piece)
        return remote(
            snd.at[way, l, rows], arr.at[way, l, rows], lane_s.at[way, l, p], lane_r.at[way, l, p], rank
        )

    def compose(way, l, p):
        rows = pl.ds(p * piece, piece)
        pick = sched[way, l]
        snd[way, l, rows] = lax.select(
            pick == chip_blocks, arr[way, l, rows], own[jnp.minimum(pick, chip_blocks - 1), rows]
        )

    def compose_own(way, l, p):
        rows = pl.ds(p * piece, piece)
        snd[way, l, rows] = own[jnp.minimum(sched[way, l], chip_blocks - 1), rows]

    def near_step(i):
        l = lanes - 1 - i
        passing = l < chip_blocks * near
        starting = jnp.logical_not(passing) & (l < chip_blocks * (near + 1))

        @pl.when((l + 2 < lanes) & (l + 2 < chip_blocks * (near + 1)))
        def _():
            for p in range(PIECES):
                lane_copy(near_way, l + 2, p, near_next).wait_send()

        @pl.when(passing)
        def _():
            for p in range(PIECES):
                lane_copy(near_way, l, p, near_next).wait_recv()
                compose(near_way, l, p)
                lane_copy(near_way, l, p, near_next).start()

        @pl.when(starting)
        def _():
            for p in range(PIECES):
                compose_own(near_way, l, p)
                lane_copy(near_way, l, p, near_next).start()

    def far_step(i):
        l = lanes - 1 - i

        @pl.when(far < chips - 1)
        def _():
            for p in range(PIECES):
                lane_copy(far_way, l, p, far_next).wait_recv()
                compose(far_way, l, p)
                lane_copy(far_way, l, p, far_next).start()

    def attend(h):
        cols = pl.ds(pl.multiple_of(h * HEAD, HEAD), HEAD)
        q = qg[:, h].reshape(2 * chips * ROWS, HEAD)
        k = kall[:, :, cols].reshape(blocks * tokens, HEAD)
        v = vall[:, :, cols].reshape(blocks * tokens, HEAD)
        s = lax.dot_general(q, k, (((1,), (1,)), ((), ())), preferred_element_type=jnp.float32)
        s = s * HEAD ** (-0.5) + bias[...]
        m = jnp.max(s, axis=1, keepdims=True)
        w = jnp.exp(s - m)
        total = jnp.sum(w, axis=1, keepdims=True)
        o = jnp.dot(w.astype(jnp.bfloat16), v, preferred_element_type=jnp.float32) / total
        part[:, h] = o.astype(jnp.bfloat16).reshape(2 * chips, ROWS, HEAD)
        lane = lax.broadcasted_iota(jnp.int32, (2 * chips, ROWS, HEAD), 2)
        level = (m + jnp.log(total)).reshape(2 * chips, ROWS, 1)
        lse[...] = jnp.where(lane == h, level, lse[...])

    near_step(0)

    for off in range(1, chips):
        other = core * chips + lax.rem(z + off, chips)
        remote(q_ref, qg.at[other], q_s.at[0], q_r.at[other], partner).wait_recv()
        remote(qg.at[other], qg.at[other], q_s.at[chips - 1 + off], q_r.at[other], partner).start()

    row_count = 2 * chips * ROWS
    row = lax.broadcasted_iota(jnp.int32, (row_count, HEAD), 0)
    slot, inner = row // ROWS, row % ROWS
    rank_row = 2 * (slot % chips) + slot // chips
    row_id = rank_row * rows_here + inner % rows_here
    valid = inner < GROUPS * rows_here
    step, request = row_id // REQ, row_id % REQ
    token = lax.broadcasted_iota(jnp.int32, (row_count, HEAD), 1)
    edge = jnp.where(valid, token + (STEPS - 1) - step, FAR)
    for s in range(blocks):
        bound = jnp.where(request == 0, limits[0, s], -FAR)
        for r in range(1, REQ):
            bound = jnp.where(request == r, limits[r, s], bound)
        bias[:, pl.ds(s * tokens, tokens)] = jnp.where(edge < bound, 0.0, LOW).astype(jnp.float32)
    lse[...] = jnp.zeros_like(lse)

    load_kp.wait()
    load_vp.wait()
    load_kc.wait()
    load_vc.wait()
    for zz in range(chips):
        other = (1 - core) * chips + zz
        remote(q_ref, qg.at[other], q_s.at[0], q_r.at[other], partner).wait_recv()

    attending = KV // HEADS_PER_STEP

    def mixed(i, carry):
        near_step(i)
        far_step(i - 1)
        for e in range(HEADS_PER_STEP):
            attend((i - 1) * HEADS_PER_STEP + e)
        return carry

    lax.fori_loop(1, 1 + attending, mixed, 0)

    theirs = pl.ds((1 - core) * chips, chips)
    s1_o = remote(part.at[theirs], pin_o, s1_s.at[0], s1_r.at[0], partner)
    s1_l = remote(lse.at[theirs], pin_l, s1_s.at[1], s1_r.at[1], partner)
    s1_o.start()
    s1_l.start()
    near_step(1 + attending)
    far_step(attending)
    s1_o.wait_recv()
    s1_l.wait_recv()

    ours = pl.ds(core * chips, chips)
    level_a, level_b = lse[ours], pin_l[...]
    top = jnp.maximum(level_a, level_b)
    ea, eb = jnp.exp(level_a - top), jnp.exp(level_b - top)
    both = ea + eb
    ml[...] = top + jnp.log(both)
    wa, wb = ea / both, eb / both
    for h in range(KV):
        pa = part[ours, h].astype(jnp.float32)
        pb = pin_o[:, h].astype(jnp.float32)
        mo[:, h] = (pa * wa[:, :, h : h + 1] + pb * wb[:, :, h : h + 1]).astype(jnp.bfloat16)
    s2 = []
    for off in range(1, chips):
        to = lax.rem(z + off, chips)
        s2.append(remote(mo.at[to], ro.at[z], s2_s.at[0, off], s2_r.at[0, z], 2 * to + core))
        s2.append(remote(ml.at[to], rl.at[z], s2_s.at[1, off], s2_r.at[1, z], 2 * to + core))
    for copy in s2:
        copy.start()
    ro[z] = mo[z]
    rl[z] = ml[z]

    def moving(i, carry):
        near_step(i)
        far_step(i - 1)
        return carry

    lax.fori_loop(2 + attending, lanes, moving, 0)
    far_step(lanes - 1)

    for off in range(1, chips):
        source = lax.rem(z + off, chips)
        remote(mo.at[source], ro.at[source], s2_s.at[0, off], s2_r.at[0, source], partner).wait_recv()
        remote(ml.at[source], rl.at[source], s2_s.at[1, off], s2_r.at[1, source], partner).wait_recv()
    levels = rl[...]
    top = jnp.max(levels, axis=0, keepdims=True)
    shares = jnp.exp(levels - top)
    shares = shares / jnp.sum(shares, axis=0, keepdims=True)
    for h in range(KV):
        att[h] = jnp.sum(ro[:, h].astype(jnp.float32) * shares[:, :, h : h + 1], axis=0).astype(jnp.bfloat16)

    @pl.when(far == chips - 1)
    def _():
        def drain(i, carry):
            for p in range(PIECES):
                lane_copy(far_way, lanes - 1 - i, p, far_next).wait_recv()
            return carry

        lax.fori_loop(0, lanes, drain, 0)

    def gathered(b, q, target):
        at_home = b // chip_blocks == z
        index = jnp.clip(b - z * chip_blocks, 0, chip_blocks - 1)
        way_of, lane_of = jnp.int32(0), jnp.int32(0)
        for way in range(2):
            for l in range(lanes):
                hit = arrivals[way][l] == b
                way_of = jnp.where(hit, way, way_of)
                lane_of = jnp.where(hit, l, lane_of)
        target[q] = lax.select(at_home, own[index], arr[way_of, lane_of])

    for q, b in enumerate(blocks_for(partner, rank_of, per_rank)):
        gathered(b, q, pout)
    handed = remote(pout, pin, fx_s, fx_r, partner)
    handed.start()
    for q, b in enumerate(blocks_for(me, rank_of, per_rank)):
        gathered(b, q, fin)

    @pl.when(core == 0)
    def _():
        pltpu.make_async_copy(fin, newk, out_s.at[0]).start()

    @pl.when(core == 1)
    def _():
        pltpu.make_async_copy(fin, newv, out_s.at[0]).start()

    handed.wait_recv()

    @pl.when(core == 0)
    def _():
        pltpu.make_async_copy(pin, newv, out_s.at[1]).start()

    @pl.when(core == 1)
    def _():
        pltpu.make_async_copy(pin, newk, out_s.at[1]).start()

    handed.wait_send()
    arrived.wait_send()
    s1_o.wait_send()
    s1_l.wait_send()
    for copy in s2:
        copy.wait_send()
    for off in range(2 * chips - 1):
        remote(q_ref, qg.at[mine], q_s.at[off], q_r.at[mine], partner).wait_send()
    for l in range(2):
        @pl.when(l < chip_blocks * (near + 1))
        def _():
            for p in range(PIECES):
                lane_copy(near_way, l, p, near_next).wait_send()

    @pl.when(far < chips - 1)
    def _():
        def sent(i, carry):
            for p in range(PIECES):
                lane_copy(far_way, i, p, far_next).wait_send()
            return carry

        lax.fori_loop(0, lanes, sent, 0)

    pltpu.make_async_copy(fin, newk, out_s.at[0]).wait()
    pltpu.make_async_copy(pin, newv, out_s.at[1]).wait()


def place_kernel(spill, first_ref, ck, cv, newk, newv, att_in, pool_k, pool_v, att_out, sem, att_sem):
    rank_slots = ck.shape[0]
    first = first_ref[0]
    att_copy = pltpu.make_async_copy(att_in, att_out, att_sem)
    att_copy.start()
    filled = [jnp.bool_(False)] * rank_slots
    count = jnp.int32(0)
    for b in range(spill.shape[0]):
        at = spill[b] - first
        mine = (at >= 0) & (at < rank_slots)
        filled = [filled[j] | (at == j) for j in range(rank_slots)]
        here, which = jnp.clip(at, 0, rank_slots - 1), jnp.minimum(count, newk.shape[0] - 1)

        @pl.when(mine)
        def _():
            pltpu.make_async_copy(newk.at[which], pool_k.at[here], sem.at[0, here]).start()
            pltpu.make_async_copy(newv.at[which], pool_v.at[here], sem.at[1, here]).start()

        count = count + mine.astype(jnp.int32)
    for j in range(rank_slots):
        @pl.when(jnp.logical_not(filled[j]))
        def _():
            pltpu.make_async_copy(ck.at[j], pool_k.at[j], sem.at[0, j]).start()
            pltpu.make_async_copy(cv.at[j], pool_v.at[j], sem.at[1, j]).start()

    for j in range(rank_slots):
        pltpu.make_async_copy(ck.at[j], pool_k.at[j], sem.at[0, j]).wait()
        pltpu.make_async_copy(cv.at[j], pool_v.at[j], sem.at[1, j]).wait()
    att_copy.wait()


def per_device(
    queries, cache_keys, pool_values_prior, prefill_keys, prefill_values, context_lengths, block_table, spill_slots
):
    ranks = lax.axis_size("blk")
    chips = ranks // 2
    me = lax.axis_index("blk")
    rank_slots, tokens, width = cache_keys.shape
    per_rank = prefill_keys.shape[0]
    chip_blocks = 2 * per_rank
    blocks = rank_slots + per_rank
    lanes = chip_blocks * (chips // 2)
    rows_here, query_width = queries.shape
    first = me * rank_slots

    held = first + jnp.arange(rank_slots, dtype=jnp.int32)
    gone = jnp.any(held[:, None] == spill_slots[None, :], axis=1)
    held = jnp.where(gone, -1, held)
    sourced = lax.dynamic_slice_in_dim(spill_slots, me * per_rank, per_rank, 0)
    targets = jnp.concatenate([held, sourced])
    columns = jnp.arange(block_table.shape[1], dtype=jnp.int32)[None, :, None]
    match = block_table[:, :, None] == targets[None, None, :]
    limits = jnp.sum(jnp.where(match, context_lengths[:, None, None] - columns * tokens + FAR, 0), axis=1) - FAR

    q = queries.reshape(rows_here, KV, GROUPS, HEAD).transpose(1, 2, 0, 3).reshape(KV, GROUPS * rows_here, HEAD)
    q = jnp.pad(q, ((0, 0), (0, ROWS - GROUPS * rows_here), (0, 0)))

    bf, f32 = jnp.bfloat16, jnp.float32
    vmem = pltpu.VMEM
    dma = pltpu.SemaphoreType.DMA
    any_spec = pl.BlockSpec(memory_space=pl.ANY)
    smem_spec = pl.BlockSpec(memory_space=pltpu.SMEM)
    vmem_spec = pl.BlockSpec(memory_space=pltpu.VMEM)
    block = (tokens, width)
    att, newk, newv = pl.pallas_call(
        functools.partial(exchange_kernel, chips, lanes),
        out_shape=(
            jax.ShapeDtypeStruct((KV, ROWS, HEAD), bf),
            jax.ShapeDtypeStruct((per_rank, *block), bf),
            jax.ShapeDtypeStruct((per_rank, *block), bf),
        ),
        in_specs=[smem_spec, smem_spec, vmem_spec] + [any_spec] * 4,
        out_specs=(vmem_spec, any_spec, any_spec),
        scratch_shapes=[
            vmem((blocks, *block), bf),
            vmem((blocks, *block), bf),
            vmem((chip_blocks, *block), bf),
            vmem((2, lanes, *block), bf),
            vmem((2, lanes, *block), bf),
            vmem((per_rank, *block), bf),
            vmem((per_rank, *block), bf),
            vmem((per_rank, *block), bf),
            vmem((ranks, KV, ROWS, HEAD), bf),
            vmem((ranks * ROWS, blocks * tokens), f32),
            vmem((ranks, KV, ROWS, HEAD), bf),
            vmem((ranks, ROWS, HEAD), f32),
            vmem((chips, KV, ROWS, HEAD), bf),
            vmem((chips, ROWS, HEAD), f32),
            vmem((chips, KV, ROWS, HEAD), bf),
            vmem((chips, ROWS, HEAD), f32),
            vmem((chips, KV, ROWS, HEAD), bf),
            vmem((chips, ROWS, HEAD), f32),
            pltpu.SMEM((2, lanes), jnp.int32),
            dma((5,)),
            dma,
            dma,
            dma((2 * chips - 1,)),
            dma((ranks,)),
            dma((2, lanes, PIECES)),
            dma((2, lanes, PIECES)),
            dma((2,)),
            dma((2,)),
            dma((2, chips)),
            dma((2, chips)),
            dma,
            dma,
            dma((2,)),
        ],
        compiler_params=pltpu.CompilerParams(
            collective_id=0, has_side_effects=True, vmem_limit_bytes=48 * 1024 * 1024
        ),
        name="exchange",
    )(limits, spill_slots, q, prefill_keys, prefill_values, cache_keys, pool_values_prior)

    pool_keys, pool_values, att = pl.pallas_call(
        place_kernel,
        out_shape=(
            jax.ShapeDtypeStruct(cache_keys.shape, bf),
            jax.ShapeDtypeStruct(cache_keys.shape, bf),
            jax.ShapeDtypeStruct(att.shape, bf),
        ),
        in_specs=[smem_spec, smem_spec] + [any_spec] * 5,
        out_specs=(any_spec,) * 3,
        scratch_shapes=[dma((2, rank_slots)), dma],
        name="place",
    )(spill_slots, first.reshape(1), cache_keys, pool_values_prior, newk, newv, att)
    attended = att[:, : GROUPS * rows_here].reshape(KV, GROUPS, rows_here, HEAD).transpose(2, 0, 1, 3)
    return attended.reshape(rows_here, query_width), pool_keys, pool_values


def solution(mesh):
    both = ("grp", "blk")
    return jax.shard_map(
        per_device,
        mesh=mesh,
        in_specs=(P(both, None),) + (P(both, None, None),) * 4 + (P("grp"), P("grp", None), P("grp")),
        out_specs=(P(both, None), P(both, None, None), P(both, None, None)),
        check_vma=False,
    )
```

time: 321 us -> 208 us (0.65)
  waiting for transfers between devices: 218 us -> 0 us
  Pallas kernels: 0 us -> 195 us
  matrix products: 41.3 us -> 0 us
  local copies, waits for them, and re-layouts: 36.8 us -> 9.51 us
  starting transfers between devices: 14.3 us -> 0 us
  other arithmetic: 8.69 us -> 2.65 us
    pallas_call x0 -> x2, Pallas kernels: none -> 195 us  [the longest x1 130 us: per_device(): pl.pallas_call(place_kernel, out_shape=(jax.ShapeDtypeStruct(cache_keys.s...]
    all_to_all x2 -> x0, waiting for transfers between devices: 174 us -> none  [the longest x1 88.2 us: per_device(): lax.all_to_all(send_keys, 'blk', split_axis=0, concat_axis=0, tiled=True)]
    ppermute x32 -> x0, waiting for transfers between devices: 44.2 us -> none  [shifted(): return lax.ppermute(value, axis, pairs)]
    dot_general x20 -> x0, matrix products: 41.3 us -> none  [the longest x8 19.2 us: local_partial(): jnp.einsum('rhgd,sthd->rhgst', query_head_rows, key_head_rows, preferred_...]
    while x35 -> x0, local copies, waits for them, and re-layouts: 13.6 us -> none
    reshape x24 -> x3, local copies, waits for them, and re-layouts: 13 us -> 1.4 us  [the longest x2 0.77 us: per_device(): queries.reshape(rows_here, KV, GROUPS, HEAD).transpose(1, 2, 0, 3)]
    all_to_all x2 -> x0, starting transfers between devices: 11.2 us -> none  [the longest x1 6.46 us: per_device(): lax.all_to_all(send_keys, 'blk', split_axis=0, concat_axis=0, tiled=True)]
    convert_element_type x4 -> x0, local copies, waits for them, and re-layouts: 9.36 us -> none  [the longest x1 4.29 us: per_device(): send_values = jnp.einsum('dqb,btw->dqtw', sending_bf, prefill_values, pre...]
  transfers between devices with their start and end apart: 34 -> 0, of which waited for: 18 -> 0; matrix products, arithmetic and copies ran while one was open for 4% -> 0% of each run, Pallas kernels for 0% -> 0%
where the time goes in v1:
time: 208 us; the launch traced here: 207 us
  Pallas kernels  195 us (94%)
  local copies, waits for them, and re-layouts  9.51 us (5%)
  other arithmetic  2.65 us (1%)
    pallas_call x1, Pallas kernels, per_device(): pl.pallas_call(place_kernel, out_shape=(jax.ShapeDtypeStruct(cache_keys.s...  130 us
    pallas_call x1, Pallas kernels, per_device(): pl.pallas_call(functools.partial(exchange_kernel, chips, lanes), out_shap...  64.5 us
    unnamed x14, local copies, waits for them, and re-layouts  6.49 us

profile of v1, /device:TPU:0, one launch (start us, length us, event | category | flops | bytes accessed | tf_op | source)
XLA Modules:
  0.0 207.4 jit_solution(13253082305198210416)
XLA Ops:
  0.6 0.7 dynamic_slice.3
  1.4 0.8 compare_reduce_fusion
  2.2 0.1 pad_add_fusion
  2.3 0.7 subtract_add_fusion
  3.0 1.0 select_reduce_fusion
  4.0 0.1 copy.17
  4.1 0.8 reshape.69
  4.9 0.0 copy-start
  4.9 1.6 copy-done
  6.5 0.0 copy-start.1
  6.5 1.0 copy-done.1
  7.6 0.0 copy-start.2
  7.6 1.0 copy-done.2
  8.6 0.0 copy-start.6
  8.6 0.7 copy-done.6
  9.3 64.5 %exchange.1 = (bf16[8,16,128]{2,1,0:T(8,128)(2,1)S(1)}, bf16[2,128,1024]{2,1,0:T(8,128)(2,1)S(1)}, bf16[2,128,1024]{2,1,0:T(8,128)(2,1)S(1)}) custom-call(s32[4,10]{1,0:T(4,128)S(1)} %broadcast_add_fusion.limits, s32[16]{0:T(128)S(1)} %copy-done.6, bf16[8,16,128]{2,1,0:T(8,128)(2,1)S(1)} %pad.4.q_ref, bf16[2,128,1024]{2,1,0:T(8,128)(2,1)S(1)} %copy-done.1, ...), custom_call_target="tpu_custom_call" | custom-call | tf_op jit(solution)/shard_map/exchange/pallas_call | solution.py:446
  73.8 0.0 copy-start.3
  73.8 0.8 copy-done.3
  74.6 0.0 copy-start.4
  74.6 0.8 copy-done.4
  75.4 0.0 copy-start.5
  75.4 0.6 copy-done.5
  76.0 130.0 %place.1 = (bf16[8,128,1024]{2,1,0:T(8,128)(2,1)}, bf16[8,128,1024]{2,1,0:T(8,128)(2,1)}, bf16[8,16,128]{2,1,0:T(8,128)(2,1)}) custom-call(s32[16]{0:T(128)} %spill.3, s32[1]{0:T(128)} %bitcast.first_ref, bf16[8,128,1024]{2,1,0:T(8,128)(2,1)} %ck.3, bf16[8,128,1024]{2,1,0:T(8,128)(2,1)} %cv.3, bf16[2,128,1024]{2,1,0:T(8,128)(2,1)} %copy-done.3, ...), custom_call_target="tpu_custom_call" | custom-call | tf_op jit(solution)/shard_map/place/pallas_call | solution.py:496
  206.0 0.8 copy.20
  206.8 0.6 reshape.72
  (8 shorter events, 0.1 us)
Async XLA Ops:
  4.9 1.6 copy-start
  6.5 1.0 copy-start.1
  7.6 1.0 copy-start.2
  8.6 0.7 copy-start.6
  73.8 0.8 copy-start.3
  74.6 0.8 copy-start.4
  75.4 0.6 copy-start.5

commit v2 on v1

--- a/solution.py
+++ b/solution.py
@@ -18,6 +18,7 @@
 HEADS_PER_STEP = 2
 LOW = -1e30
 FAR = 1 << 24
+VMEM_BYTES = 60 * 1024 * 1024
 MESH = pl.DeviceIdType.MESH
 
 
@@ -67,9 +68,9 @@
 
 
 def exchange_kernel(
-    chips, lanes, limits, spill, q_ref, pk, pv, ck, cv,
+    chips, lanes, lengths, table, spill, q_in, pk, pv, ck, cv,
     att, newk, newv,
-    kall, vall, own, arr, snd, fin, pout, pin, qg, bias, part, lse, pin_o, pin_l, mo, ml, ro, rl, sched,
+    kall, vall, own, arr, snd, fin, pout, pin, qg, bias, part, lse, pin_o, pin_l, mo, ml, ro, rl, sched, q_wide, q_ref, att_wide,
     loc, ex_s, ex_r, q_s, q_r, lane_s, lane_r, s1_s, s1_r, s2_s, s2_r, fx_s, fx_r, out_s,
 ):
     rank_slots, tokens, width = ck.shape
@@ -123,6 +124,14 @@
         remote(pk, own_mine, ex_s, ex_r, partner).start()
 
     mine = core * chips + z
+    q_wide[...] = jnp.zeros_like(q_wide)
+    q_rows = q_in[...].astype(jnp.float32)
+    for h in range(KV):
+        for j in range(GROUPS * rows_here):
+            head = h * GROUPS + j // rows_here
+            i = j % rows_here
+            q_wide[h, j : j + 1, :] = q_rows[i : i + 1, head * HEAD : (head + 1) * HEAD]
+    q_ref[...] = q_wide[...].astype(jnp.bfloat16)
     q_copies = [remote(q_ref, qg.at[mine], q_s.at[0], q_r.at[mine], partner)]
     for off in range(1, chips):
         peer = 2 * lax.rem(z + off, chips) + core
@@ -210,7 +219,7 @@
         w = jnp.exp(s - m)
         total = jnp.sum(w, axis=1, keepdims=True)
         o = jnp.dot(w.astype(jnp.bfloat16), v, preferred_element_type=jnp.float32) / total
-        part[:, h] = o.astype(jnp.bfloat16).reshape(2 * chips, ROWS, HEAD)
+        part[:, h] = o.reshape(2 * chips, ROWS, HEAD)
         lane = lax.broadcasted_iota(jnp.int32, (2 * chips, ROWS, HEAD), 2)
         level = (m + jnp.log(total)).reshape(2 * chips, ROWS, 1)
         lse[...] = jnp.where(lane == h, level, lse[...])
@@ -230,11 +239,23 @@
     valid = inner < GROUPS * rows_here
     step, request = row_id // REQ, row_id % REQ
     token = lax.broadcasted_iota(jnp.int32, (row_count, HEAD), 1)
-    edge = jnp.where(valid, token + (STEPS - 1) - step, FAR)
+    edge = jnp.where(valid, token + (STEPS - 1) - step, FAR).astype(jnp.float32)
+    columns = table.shape[1]
+    owned = jnp.broadcast_to(table[0:1, :], (row_count, columns))
+    length = jnp.full((row_count, columns), lengths[0], jnp.int32)
+    for r in range(1, REQ):
+        here = request[:, :columns] == r
+        owned = jnp.where(here, table[r : r + 1, :], owned)
+        length = jnp.where(here, lengths[r], length)
+    after = (length - lax.broadcasted_iota(jnp.int32, (row_count, columns), 1) * tokens).astype(jnp.float32)
     for s in range(blocks):
-        bound = jnp.where(request == 0, limits[0, s], -FAR)
-        for r in range(1, REQ):
-            bound = jnp.where(request == r, limits[r, s], bound)
+        if s < rank_slots:
+            block_id = me * rank_slots + s
+            for b in range(chips * chip_blocks):
+                block_id = jnp.where(spill[b] == me * rank_slots + s, -1, block_id)
+        else:
+            block_id = spill[me * per_rank + s - rank_slots]
+        bound = jnp.max(jnp.where(owned == block_id, after, float(-FAR)), axis=1, keepdims=True)
         bias[:, pl.ds(s * tokens, tokens)] = jnp.where(edge < bound, 0.0, LOW).astype(jnp.float32)
     lse[...] = jnp.zeros_like(lse)
 
@@ -275,9 +296,8 @@
     ml[...] = top + jnp.log(both)
     wa, wb = ea / both, eb / both
     for h in range(KV):
-        pa = part[ours, h].astype(jnp.float32)
-        pb = pin_o[:, h].astype(jnp.float32)
-        mo[:, h] = (pa * wa[:, :, h : h + 1] + pb * wb[:, :, h : h + 1]).astype(jnp.bfloat16)
+        mixed_rows = part[ours, h] * wa[:, :, h : h + 1] + pin_o[:, h] * wb[:, :, h : h + 1]
+        mo[:, h] = mixed_rows.astype(jnp.bfloat16)
     s2 = []
     for off in range(1, chips):
         to = lax.rem(z + off, chips)
@@ -305,7 +325,12 @@
     shares = jnp.exp(levels - top)
     shares = shares / jnp.sum(shares, axis=0, keepdims=True)
     for h in range(KV):
-        att[h] = jnp.sum(ro[:, h].astype(jnp.float32) * shares[:, :, h : h + 1], axis=0).astype(jnp.bfloat16)
+        rows = jnp.sum(ro[:, h].astype(jnp.float32) * shares[:, :, h : h + 1], axis=0)
+        for j in range(GROUPS * rows_here):
+            head = h * GROUPS + j // rows_here
+            i = j % rows_here
+            att_wide[i : i + 1, head * HEAD : (head + 1) * HEAD] = rows[j : j + 1, :]
+    att[...] = att_wide[...].astype(jnp.bfloat16)
 
     @pl.when(far == chips - 1)
     def _():
@@ -379,11 +404,9 @@
     pltpu.make_async_copy(pin, newv, out_s.at[1]).wait()
 
 
-def place_kernel(spill, first_ref, ck, cv, newk, newv, att_in, pool_k, pool_v, att_out, sem, att_sem):
+def place_kernel(spill, first_ref, ck, cv, newk, newv, att_in, pool_k, pool_v, att_out, hold, into, out):
     rank_slots = ck.shape[0]
     first = first_ref[0]
-    att_copy = pltpu.make_async_copy(att_in, att_out, att_sem)
-    att_copy.start()
     filled = [jnp.bool_(False)] * rank_slots
     count = jnp.int32(0)
     for b in range(spill.shape[0]):
@@ -394,20 +417,25 @@
 
         @pl.when(mine)
         def _():
-            pltpu.make_async_copy(newk.at[which], pool_k.at[here], sem.at[0, here]).start()
-            pltpu.make_async_copy(newv.at[which], pool_v.at[here], sem.at[1, here]).start()
+            pltpu.make_async_copy(newk.at[which], hold.at[0, here], into.at[0, here]).start()
+            pltpu.make_async_copy(newv.at[which], hold.at[1, here], into.at[1, here]).start()
 
         count = count + mine.astype(jnp.int32)
     for j in range(rank_slots):
         @pl.when(jnp.logical_not(filled[j]))
         def _():
-            pltpu.make_async_copy(ck.at[j], pool_k.at[j], sem.at[0, j]).start()
-            pltpu.make_async_copy(cv.at[j], pool_v.at[j], sem.at[1, j]).start()
-
+            pltpu.make_async_copy(ck.at[j], hold.at[0, j], into.at[0, j]).start()
+            pltpu.make_async_copy(cv.at[j], hold.at[1, j], into.at[1, j]).start()
+
+    att_out[...] = att_in[...]
+    stores = []
     for j in range(rank_slots):
-        pltpu.make_async_copy(ck.at[j], pool_k.at[j], sem.at[0, j]).wait()
-        pltpu.make_async_copy(cv.at[j], pool_v.at[j], sem.at[1, j]).wait()
-    att_copy.wait()
+        for t, (source, target) in enumerate(((ck, pool_k), (cv, pool_v))):
+            pltpu.make_async_copy(source.at[j], hold.at[t, j], into.at[t, j]).wait()
+            stores.append(pltpu.make_async_copy(hold.at[t, j], target.at[j], out.at[t, j]))
+            stores[-1].start()
+    for copy in stores:
+        copy.wait()
 
 
 def per_device(
@@ -424,18 +452,6 @@
     rows_here, query_width = queries.shape
     first = me * rank_slots
 
-    held = first + jnp.arange(rank_slots, dtype=jnp.int32)
-    gone = jnp.any(held[:, None] == spill_slots[None, :], axis=1)
-    held = jnp.where(gone, -1, held)
-    sourced = lax.dynamic_slice_in_dim(spill_slots, me * per_rank, per_rank, 0)
-    targets = jnp.concatenate([held, sourced])
-    columns = jnp.arange(block_table.shape[1], dtype=jnp.int32)[None, :, None]
-    match = block_table[:, :, None] == targets[None, None, :]
-    limits = jnp.sum(jnp.where(match, context_lengths[:, None, None] - columns * tokens + FAR, 0), axis=1) - FAR
-
-    q = queries.reshape(rows_here, KV, GROUPS, HEAD).transpose(1, 2, 0, 3).reshape(KV, GROUPS * rows_here, HEAD)
-    q = jnp.pad(q, ((0, 0), (0, ROWS - GROUPS * rows_here), (0, 0)))
-
     bf, f32 = jnp.bfloat16, jnp.float32
     vmem = pltpu.VMEM
     dma = pltpu.SemaphoreType.DMA
@@ -446,11 +462,11 @@
     att, newk, newv = pl.pallas_call(
         functools.partial(exchange_kernel, chips, lanes),
         out_shape=(
-            jax.ShapeDtypeStruct((KV, ROWS, HEAD), bf),
+            jax.ShapeDtypeStruct(queries.shape, bf),
             jax.ShapeDtypeStruct((per_rank, *block), bf),
             jax.ShapeDtypeStruct((per_rank, *block), bf),
         ),
-        in_specs=[smem_spec, smem_spec, vmem_spec] + [any_spec] * 4,
+        in_specs=[smem_spec, vmem_spec, smem_spec, vmem_spec] + [any_spec] * 4,
         out_specs=(vmem_spec, any_spec, any_spec),
         scratch_shapes=[
             vmem((blocks, *block), bf),
@@ -463,15 +479,18 @@
             vmem((per_rank, *block), bf),
             vmem((ranks, KV, ROWS, HEAD), bf),
             vmem((ranks * ROWS, blocks * tokens), f32),
-            vmem((ranks, KV, ROWS, HEAD), bf),
+            vmem((ranks, KV, ROWS, HEAD), f32),
             vmem((ranks, ROWS, HEAD), f32),
-            vmem((chips, KV, ROWS, HEAD), bf),
+            vmem((chips, KV, ROWS, HEAD), f32),
             vmem((chips, ROWS, HEAD), f32),
             vmem((chips, KV, ROWS, HEAD), bf),
             vmem((chips, ROWS, HEAD), f32),
             vmem((chips, KV, ROWS, HEAD), bf),
             vmem((chips, ROWS, HEAD), f32),
             pltpu.SMEM((2, lanes), jnp.int32),
+            vmem((KV, ROWS, HEAD), f32),
+            vmem((KV, ROWS, HEAD), bf),
+            vmem(queries.shape, f32),
             dma((5,)),
             dma,
             dma,
@@ -488,10 +507,10 @@
             dma((2,)),
         ],
         compiler_params=pltpu.CompilerParams(
-            collective_id=0, has_side_effects=True, vmem_limit_bytes=48 * 1024 * 1024
+            collective_id=0, has_side_effects=True, vmem_limit_bytes=VMEM_BYTES
         ),
         name="exchange",
-    )(limits, spill_slots, q, prefill_keys, prefill_values, cache_keys, pool_values_prior)
+    )(context_lengths, block_table, spill_slots, queries, prefill_keys, prefill_values, cache_keys, pool_values_prior)
 
     pool_keys, pool_values, att = pl.pallas_call(
         place_kernel,
@@ -500,13 +519,13 @@
             jax.ShapeDtypeStruct(cache_keys.shape, bf),
             jax.ShapeDtypeStruct(att.shape, bf),
         ),
-        in_specs=[smem_spec, smem_spec] + [any_spec] * 5,
-        out_specs=(any_spec,) * 3,
-        scratch_shapes=[dma((2, rank_slots)), dma],
+        in_specs=[smem_spec, smem_spec] + [any_spec] * 4 + [vmem_spec],
+        out_specs=(any_spec, any_spec, vmem_spec),
+        scratch_shapes=[vmem((2, rank_slots, *block), bf), dma((2, rank_slots)), dma((2, rank_slots))],
+        compiler_params=pltpu.CompilerParams(vmem_limit_bytes=VMEM_BYTES),
         name="place",
     )(spill_slots, first.reshape(1), cache_keys, pool_values_prior, newk, newv, att)
-    attended = att[:, : GROUPS * rows_here].reshape(KV, GROUPS, rows_here, HEAD).transpose(2, 0, 1, 3)
-    return attended.reshape(rows_here, query_width), pool_keys, pool_values
+    return att, pool_keys, pool_values
 
 
 def solution(mesh):

time: 208 us -> 71.5 us (0.34)
  Pallas kernels: 195 us -> 70.1 us
  local copies, waits for them, and re-layouts: 9.51 us -> 0 us
  other arithmetic: 2.65 us -> 0 us
    pallas_call x1, Pallas kernels: 130 us -> 4.94 us  [per_device(): pl.pallas_call(place_kernel, out_shape=(jax.ShapeDtypeStruct(cache_keys.s...]
    unnamed x14 -> x0, local copies, waits for them, and re-layouts: 6.49 us -> none
where the time goes in v2:
time: 71.5 us; the launch traced here: 70.8 us
  Pallas kernels  70.1 us (98%)
    pallas_call x1, Pallas kernels, per_device(): pl.pallas_call(functools.partial(exchange_kernel, chips, lanes), out_shap...  65.2 us
    pallas_call x1, Pallas kernels, per_device(): pl.pallas_call(place_kernel, out_shape=(jax.ShapeDtypeStruct(cache_keys.s...  4.94 us

profile of v2, /device:TPU:0, one launch (start us, length us, event | category | flops | bytes accessed | tf_op | source)
XLA Modules:
  0.0 70.8 jit_solution(13203887575878963216)
XLA Ops:
  0.6 65.2 %exchange.1 = (bf16[2,5120]{1,0:T(2,128)(2,1)}, bf16[2,128,1024]{2,1,0:T(8,128)(2,1)}, bf16[2,128,1024]{2,1,0:T(8,128)(2,1)}) custom-call(s32[4]{0:T(128)} %lengths.1, s32[4,16]{1,0:T(4,128)} %table.1, s32[16]{0:T(128)} %spill.3, bf16[2,5120]{1,0:T(2,128)(2,1)} %q_in.1, bf16[2,128,1024]{2,1,0:T(8,128)(2,1)} %pk.1, bf16[2,128,1024]{2,1,0:T(8,128)(2,1)} %pv.1, ...), custom_call_target="tpu_custom_call" | custom-call | tf_op jit(solution)/shard_map/exchange/pallas_call | solution.py:462
  65.8 4.9 %place.1 = (bf16[8,128,1024]{2,1,0:T(8,128)(2,1)}, bf16[8,128,1024]{2,1,0:T(8,128)(2,1)}, bf16[2,5120]{1,0:T(2,128)(2,1)}) custom-call(s32[16]{0:T(128)} %spill.3, s32[1]{0:T(128)} %bitcast.first_ref, bf16[8,128,1024]{2,1,0:T(8,128)(2,1)} %ck.3, bf16[8,128,1024]{2,1,0:T(8,128)(2,1)} %cv.3, bf16[2,128,1024]{2,1,0:T(8,128)(2,1)} %get-tuple-element.9.newk, ...), custom_call_target="tpu_custom_call" | custom-call | tf_op jit(solution)/shard_map/place/pallas_call | solution.py:515

commit v3 on v2

--- a/solution.py
+++ b/solution.py
@@ -177,10 +177,12 @@
 
     def near_step(i):
         l = lanes - 1 - i
-        passing = l < chip_blocks * near
-        starting = jnp.logical_not(passing) & (l < chip_blocks * (near + 1))
-
-        @pl.when((l + 2 < lanes) & (l + 2 < chip_blocks * (near + 1)))
+        if isinstance(i, int) and l < 0:
+            return
+        passing = (l >= 0) & (l < chip_blocks * near)
+        starting = (l >= 0) & jnp.logical_not(passing) & (l < chip_blocks * (near + 1))
+
+        @pl.when((l >= 0) & (l + 2 < lanes) & (l + 2 < chip_blocks * (near + 1)))
         def _():
             for p in range(PIECES):
                 lane_copy(near_way, l + 2, p, near_next).wait_send()
@@ -200,8 +202,10 @@
 
     def far_step(i):
         l = lanes - 1 - i
-
-        @pl.when(far < chips - 1)
+        if isinstance(i, int) and l < 0:
+            return
+
+        @pl.when((l >= 0) & (far < chips - 1))
         def _():
             for p in range(PIECES):
                 lane_copy(far_way, l, p, far_next).wait_recv()
@@ -313,8 +317,10 @@
         far_step(i - 1)
         return carry
 
-    lax.fori_loop(2 + attending, lanes, moving, 0)
-    far_step(lanes - 1)
+    if lanes > 2 + attending:
+        lax.fori_loop(2 + attending, lanes, moving, 0)
+    if lanes > 1 + attending:
+        far_step(lanes - 1)
 
     for off in range(1, chips):
         source = lax.rem(z + off, chips)
@@ -404,6 +410,42 @@
     pltpu.make_async_copy(pin, newv, out_s.at[1]).wait()
 
 
+def load_kernel(chips, chip_blocks, rank_slots, steps, spill, pick, box, send, recv):
+    groups = lax.axis_size("grp")
+    mine = lax.axis_index("grp")
+    barrier = pltpu.get_barrier_semaphore()
+    for off in range(1, groups):
+        peer = lax.rem(mine + off, groups)
+        pl.semaphore_signal(barrier, inc=1, device_id={"grp": peer}, device_id_type=MESH)
+    chip_of = [spill[b] // (2 * rank_slots) for b in range(chips * chip_blocks)]
+    load = jnp.int32(0)
+    for n in range(chips - 1):
+        crossing = jnp.int32(0)
+        for b in range((n + 1) * chip_blocks):
+            crossing = crossing + (chip_of[b] > n).astype(jnp.int32)
+        load = jnp.maximum(load, crossing)
+    box[mine] = jnp.full(box.shape[1:], load, jnp.int32)
+    pl.semaphore_wait(barrier, groups - 1)
+
+    def copy_to(off, source):
+        return pltpu.make_async_remote_copy(
+            src_ref=box.at[mine], dst_ref=box.at[mine], send_sem=send.at[off], recv_sem=recv.at[source],
+            device_id={"grp": lax.rem(mine + off, groups)}, device_id_type=MESH,
+        )
+
+    for off in range(1, groups):
+        copy_to(off, mine).start()
+    for off in range(1, groups):
+        copy_to(off, lax.rem(mine + off, groups)).wait_recv()
+    largest = jnp.max(box[...])
+    choice = jnp.int32(0)
+    for step in steps[:-1]:
+        choice = choice + (largest > step).astype(jnp.int32)
+    pick[0] = choice
+    for off in range(1, groups):
+        copy_to(off, mine).wait_send()
+
+
 def place_kernel(spill, first_ref, ck, cv, newk, newv, att_in, pool_k, pool_v, att_out, hold, into, out):
     rank_slots = ck.shape[0]
     first = first_ref[0]
@@ -448,7 +490,8 @@
     per_rank = prefill_keys.shape[0]
     chip_blocks = 2 * per_rank
     blocks = rank_slots + per_rank
-    lanes = chip_blocks * (chips // 2)
+    most = chip_blocks * (chips // 2)
+    choices = (most // 2, most * 5 // 8, most * 3 // 4, most)
     rows_here, query_width = queries.shape
     first = me * rank_slots
 
@@ -459,58 +502,78 @@
     smem_spec = pl.BlockSpec(memory_space=pltpu.SMEM)
     vmem_spec = pl.BlockSpec(memory_space=pltpu.VMEM)
     block = (tokens, width)
-    att, newk, newv = pl.pallas_call(
-        functools.partial(exchange_kernel, chips, lanes),
-        out_shape=(
-            jax.ShapeDtypeStruct(queries.shape, bf),
-            jax.ShapeDtypeStruct((per_rank, *block), bf),
-            jax.ShapeDtypeStruct((per_rank, *block), bf),
-        ),
-        in_specs=[smem_spec, vmem_spec, smem_spec, vmem_spec] + [any_spec] * 4,
-        out_specs=(vmem_spec, any_spec, any_spec),
+    def exchange(number, lanes, *operands):
+        return pl.pallas_call(
+            functools.partial(exchange_kernel, chips, lanes),
+            out_shape=(
+                jax.ShapeDtypeStruct(queries.shape, bf),
+                jax.ShapeDtypeStruct((per_rank, *block), bf),
+                jax.ShapeDtypeStruct((per_rank, *block), bf),
+            ),
+            in_specs=[smem_spec, vmem_spec, smem_spec, vmem_spec] + [any_spec] * 4,
+            out_specs=(vmem_spec, any_spec, any_spec),
+            scratch_shapes=[
+                vmem((blocks, *block), bf),
+                vmem((blocks, *block), bf),
+                vmem((chip_blocks, *block), bf),
+                vmem((2, lanes, *block), bf),
+                vmem((2, lanes, *block), bf),
+                vmem((per_rank, *block), bf),
+                vmem((per_rank, *block), bf),
+                vmem((per_rank, *block), bf),
+                vmem((ranks, KV, ROWS, HEAD), bf),
+                vmem((ranks * ROWS, blocks * tokens), f32),
+                vmem((ranks, KV, ROWS, HEAD), f32),
+                vmem((ranks, ROWS, HEAD), f32),
+                vmem((chips, KV, ROWS, HEAD), f32),
+                vmem((chips, ROWS, HEAD), f32),
+                vmem((chips, KV, ROWS, HEAD), bf),
+                vmem((chips, ROWS, HEAD), f32),
+                vmem((chips, KV, ROWS, HEAD), bf),
+                vmem((chips, ROWS, HEAD), f32),
+                pltpu.SMEM((2, lanes), jnp.int32),
+                vmem((KV, ROWS, HEAD), f32),
+                vmem((KV, ROWS, HEAD), bf),
+                vmem(queries.shape, f32),
+                dma((5,)),
+                dma,
+                dma,
+                dma((2 * chips - 1,)),
+                dma((ranks,)),
+                dma((2, lanes, PIECES)),
+                dma((2, lanes, PIECES)),
+                dma((2,)),
+                dma((2,)),
+                dma((2, chips)),
+                dma((2, chips)),
+                dma,
+                dma,
+                dma((2,)),
+            ],
+            compiler_params=pltpu.CompilerParams(
+                collective_id=1 + number, has_side_effects=True, vmem_limit_bytes=VMEM_BYTES
+            ),
+            name="exchange",
+        )(*operands)
+
+    pick = pl.pallas_call(
+        functools.partial(load_kernel, chips, chip_blocks, rank_slots, choices),
+        out_shape=jax.ShapeDtypeStruct((1,), jnp.int32),
+        in_specs=[smem_spec],
+        out_specs=smem_spec,
         scratch_shapes=[
-            vmem((blocks, *block), bf),
-            vmem((blocks, *block), bf),
-            vmem((chip_blocks, *block), bf),
-            vmem((2, lanes, *block), bf),
-            vmem((2, lanes, *block), bf),
-            vmem((per_rank, *block), bf),
-            vmem((per_rank, *block), bf),
-            vmem((per_rank, *block), bf),
-            vmem((ranks, KV, ROWS, HEAD), bf),
-            vmem((ranks * ROWS, blocks * tokens), f32),
-            vmem((ranks, KV, ROWS, HEAD), f32),
-            vmem((ranks, ROWS, HEAD), f32),
-            vmem((chips, KV, ROWS, HEAD), f32),
-            vmem((chips, ROWS, HEAD), f32),
-            vmem((chips, KV, ROWS, HEAD), bf),
-            vmem((chips, ROWS, HEAD), f32),
-            vmem((chips, KV, ROWS, HEAD), bf),
-            vmem((chips, ROWS, HEAD), f32),
-            pltpu.SMEM((2, lanes), jnp.int32),
-            vmem((KV, ROWS, HEAD), f32),
-            vmem((KV, ROWS, HEAD), bf),
-            vmem(queries.shape, f32),
-            dma((5,)),
-            dma,
-            dma,
-            dma((2 * chips - 1,)),
-            dma((ranks,)),
-            dma((2, lanes, PIECES)),
-            dma((2, lanes, PIECES)),
-            dma((2,)),
-            dma((2,)),
-            dma((2, chips)),
-            dma((2, chips)),
-            dma,
-            dma,
-            dma((2,)),
+            vmem((lax.axis_size("grp"), 8, HEAD), jnp.int32),
+            dma((lax.axis_size("grp"),)),
+            dma((lax.axis_size("grp"),)),
         ],
-        compiler_params=pltpu.CompilerParams(
-            collective_id=0, has_side_effects=True, vmem_limit_bytes=VMEM_BYTES
-        ),
-        name="exchange",
-    )(context_lengths, block_table, spill_slots, queries, prefill_keys, prefill_values, cache_keys, pool_values_prior)
+        compiler_params=pltpu.CompilerParams(collective_id=0, has_side_effects=True),
+        name="load",
+    )(spill_slots)
+    att, newk, newv = lax.switch(
+        pick[0],
+        [functools.partial(exchange, number, lanes) for number, lanes in enumerate(choices)],
+        context_lengths, block_table, spill_slots, queries, prefill_keys, prefill_values, cache_keys, pool_values_prior,
+    )
 
     pool_keys, pool_values, att = pl.pallas_call(
         place_kernel,

time: 71.5 us -> 66.6 us (0.931)
  Pallas kernels: 70.1 us -> 64.6 us
  between operations: 0.64 us -> 1.45 us
    pallas_call x1 -> x2, Pallas kernels: 65.2 us -> 59.8 us  [the longest x1 52.2 us: exchange(): pl.pallas_call(functools.partial(exchange_kernel, chips, lanes), out_shap...]
where the time goes in v3:
time: 66.6 us; the launch traced here: 66.4 us
  Pallas kernels  64.6 us (97%)
  between operations  1.45 us (2%)
    pallas_call x1, Pallas kernels, exchange(): pl.pallas_call(functools.partial(exchange_kernel, chips, lanes), out_shap...  52.2 us
    pallas_call x1, Pallas kernels, per_device(): pl.pallas_call(functools.partial(load_kernel, chips, chip_blocks, rank_sl...  7.59 us
    pallas_call x1, Pallas kernels, per_device(): pl.pallas_call(place_kernel, out_shape=(jax.ShapeDtypeStruct(cache_keys.s...  4.88 us

profile of v3, /device:TPU:0, one launch (start us, length us, event | category | flops | bytes accessed | tf_op | source)
XLA Modules:
  0.0 66.4 jit_solution(17235050881431742622)
XLA Ops:
  0.6 7.6 %load.1 = s32[1]{0:T(128)} custom-call(s32[16]{0:T(128)} %spill.3), custom_call_target="tpu_custom_call" | custom-call | tf_op jit(solution)/shard_map/load/pallas_call | solution.py:559
  8.8 52.4 %conditional.1 = ((bf16[2,5120]{1,0:T(2,128)(2,1)S(1)}, bf16[2,128,1024]{2,1,0:T(8,128)(2,1)S(1)}, bf16[2,128,1024]{2,1,0:T(8,128)(2,1)S(1)})) conditional(s32[]{:T(128)} %bitcast.1, (s32[4]{0:T(128)}, s32[4,16]{1,0:T(4,128)}, s32[16]{0:T(128)}, bf16[2,5120]{1,0:T(2,128)(2,1)}, bf16[2,128,1024]{2,1,0:T(8,128)(2,1)}, ...), branch_computations={%region_0.0_spmd, %region_1.0_spmd, %region_2.0_spmd, %region_3.0_... | conditional | bytes 8 | solution.py:572
  8.9 52.2 %exchange.5 = (bf16[2,5120]{1,0:T(2,128)(2,1)S(1)}, bf16[2,128,1024]{2,1,0:T(8,128)(2,1)S(1)}, bf16[2,128,1024]{2,1,0:T(8,128)(2,1)S(1)}) custom-call(s32[4]{0:T(128)} %get-tuple-element.72.lengths, s32[4,16]{1,0:T(4,128)} %get-tuple-element.73.table, s32[16]{0:T(128)} %get-tuple-element.74.spill, bf16[2,5120]{1,0:T(2,128)(2,1)} %get-tuple-element.75.q_in, ...), custom_call_target="tpu_custom_call" | custom-call | tf_op jit(solution)/shard_map/cond/branch_1_fun/exchange/pallas_call | solution.py:506
  61.3 4.9 %place.1 = (bf16[8,128,1024]{2,1,0:T(8,128)(2,1)}, bf16[8,128,1024]{2,1,0:T(8,128)(2,1)}, bf16[2,5120]{1,0:T(2,128)(2,1)}) custom-call(s32[16]{0:T(128)} %spill.3, s32[1]{0:T(128)} %bitcast.first_ref, bf16[8,128,1024]{2,1,0:T(8,128)(2,1)} %ck.1, bf16[8,128,1024]{2,1,0:T(8,128)(2,1)} %cv.1, bf16[2,128,1024]{2,1,0:T(8,128)(2,1)S(1)} %get-tuple-element.105.newk, ...), custom_call_target="tpu_custom_call" | custom-call | tf_op jit(solution)/shard_map/place/pallas_call | solution.py:578

commit v4 on v3

--- a/solution.py
+++ b/solution.py
@@ -14,7 +14,7 @@
 STEPS = 4
 REQ = 4
 ROWS = 16
-PIECES = 4
+PIECES = 8
 HEADS_PER_STEP = 2
 LOW = -1e30
 FAR = 1 << 24
@@ -68,10 +68,10 @@
 
 
 def exchange_kernel(
-    chips, lanes, lengths, table, spill, q_in, pk, pv, ck, cv,
+    chips, lanes, lengths, table, spill, qg, other, pk, pv, ck, cv,
     att, newk, newv,
-    kall, vall, own, arr, snd, fin, pout, pin, qg, bias, part, lse, pin_o, pin_l, mo, ml, ro, rl, sched, q_wide, q_ref, att_wide,
-    loc, ex_s, ex_r, q_s, q_r, lane_s, lane_r, s1_s, s1_r, s2_s, s2_r, fx_s, fx_r, out_s,
+    kall, vall, own, arr, snd, fin, pout, bias, part, lse, pin_o, pin_l, mo, ml, ro, rl, sched, att_wide,
+    loc, lane_s, lane_r, s1_s, s1_r, s2_s, s2_r, fx_s, fx_r, out_s,
 ):
     rank_slots, tokens, width = ck.shape
     per_rank = pk.shape[0]
@@ -103,6 +103,8 @@
     def _():
         pltpu.make_async_copy(pv, own_mine, loc.at[4]).start()
 
+    load_other = pltpu.make_async_copy(other, own.at[pl.ds((1 - core) * per_rank, per_rank)], loc.at[5])
+    load_other.start()
     load_kp.start()
     load_vp.start()
     load_kc.start()
@@ -113,42 +115,13 @@
     for off in range(1, chips):
         peer = 2 * lax.rem(z + off, chips) + core
         pl.semaphore_signal(barrier, inc=1, device_id={"blk": peer}, device_id_type=MESH)
-    pl.semaphore_wait(barrier, chips)
-
-    @pl.when(core == 0)
-    def _():
-        remote(pv, own_mine, ex_s, ex_r, partner).start()
-
-    @pl.when(core == 1)
-    def _():
-        remote(pk, own_mine, ex_s, ex_r, partner).start()
-
-    mine = core * chips + z
-    q_wide[...] = jnp.zeros_like(q_wide)
-    q_rows = q_in[...].astype(jnp.float32)
-    for h in range(KV):
-        for j in range(GROUPS * rows_here):
-            head = h * GROUPS + j // rows_here
-            i = j % rows_here
-            q_wide[h, j : j + 1, :] = q_rows[i : i + 1, head * HEAD : (head + 1) * HEAD]
-    q_ref[...] = q_wide[...].astype(jnp.bfloat16)
-    q_copies = [remote(q_ref, qg.at[mine], q_s.at[0], q_r.at[mine], partner)]
-    for off in range(1, chips):
-        peer = 2 * lax.rem(z + off, chips) + core
-        q_copies.append(remote(q_ref, qg.at[mine], q_s.at[off], q_r.at[mine], peer))
-    for copy in q_copies:
-        copy.start()
-    qg[mine] = q_ref[...]
-
     rank_of, sends, arrivals = lane_plan(spill, chips, z, lanes, chip_blocks, rank_slots)
     for way in range(2):
         for l in range(lanes):
             sched[way, l] = sends[way][l]
-
     pltpu.make_async_copy(pk, own_mine, loc.at[4]).wait()
-    own_other = own.at[pl.ds((1 - core) * per_rank, per_rank)]
-    arrived = remote(pk, own_other, ex_s, ex_r, partner)
-    arrived.wait_recv()
+    load_other.wait()
+    pl.semaphore_wait(barrier, chips)
 
     low_half = z < chips // 2
     near = jnp.where(low_half, z, chips - 1 - z)
@@ -229,11 +202,6 @@
         lse[...] = jnp.where(lane == h, level, lse[...])
 
     near_step(0)
-
-    for off in range(1, chips):
-        other = core * chips + lax.rem(z + off, chips)
-        remote(q_ref, qg.at[other], q_s.at[0], q_r.at[other], partner).wait_recv()
-        remote(qg.at[other], qg.at[other], q_s.at[chips - 1 + off], q_r.at[other], partner).start()
 
     row_count = 2 * chips * ROWS
     row = lax.broadcasted_iota(jnp.int32, (row_count, HEAD), 0)
@@ -267,9 +235,6 @@
     load_vp.wait()
     load_kc.wait()
     load_vc.wait()
-    for zz in range(chips):
-        other = (1 - core) * chips + zz
-        remote(q_ref, qg.at[other], q_s.at[0], q_r.at[other], partner).wait_recv()
 
     attending = KV // HEADS_PER_STEP
 
@@ -322,6 +287,49 @@
     if lanes > 1 + attending:
         far_step(lanes - 1)
 
+    @pl.when(far == chips - 1)
+    def _():
+        def drain(i, carry):
+            for p in range(PIECES):
+                lane_copy(far_way, lanes - 1 - i, p, far_next).wait_recv()
+            return carry
+
+        lax.fori_loop(0, lanes, drain, 0)
+
+    def gathered(b, q, target):
+        at_home = b // chip_blocks == z
+        index = jnp.clip(b - z * chip_blocks, 0, chip_blocks - 1)
+        way_of, lane_of = jnp.int32(0), jnp.int32(0)
+        for way in range(2):
+            for l in range(lanes):
+                hit = arrivals[way][l] == b
+                way_of = jnp.where(hit, way, way_of)
+                lane_of = jnp.where(hit, l, lane_of)
+        target[q] = lax.select(at_home, own[index], arr[way_of, lane_of])
+
+    for q, b in enumerate(blocks_for(partner, rank_of, per_rank)):
+        gathered(b, q, pout)
+    handed = remote(pout, newk, fx_s, fx_r, partner)
+
+    @pl.when(core == 0)
+    def _():
+        handed.start()
+
+    @pl.when(core == 1)
+    def _():
+        remote(pout, newv, fx_s, fx_r, partner).start()
+
+    for q, b in enumerate(blocks_for(me, rank_of, per_rank)):
+        gathered(b, q, fin)
+
+    @pl.when(core == 0)
+    def _():
+        pltpu.make_async_copy(fin, newk, out_s).start()
+
+    @pl.when(core == 1)
+    def _():
+        pltpu.make_async_copy(fin, newv, out_s).start()
+
     for off in range(1, chips):
         source = lax.rem(z + off, chips)
         remote(mo.at[source], ro.at[source], s2_s.at[0, off], s2_r.at[0, source], partner).wait_recv()
@@ -338,59 +346,13 @@
             att_wide[i : i + 1, head * HEAD : (head + 1) * HEAD] = rows[j : j + 1, :]
     att[...] = att_wide[...].astype(jnp.bfloat16)
 
-    @pl.when(far == chips - 1)
-    def _():
-        def drain(i, carry):
-            for p in range(PIECES):
-                lane_copy(far_way, lanes - 1 - i, p, far_next).wait_recv()
-            return carry
-
-        lax.fori_loop(0, lanes, drain, 0)
-
-    def gathered(b, q, target):
-        at_home = b // chip_blocks == z
-        index = jnp.clip(b - z * chip_blocks, 0, chip_blocks - 1)
-        way_of, lane_of = jnp.int32(0), jnp.int32(0)
-        for way in range(2):
-            for l in range(lanes):
-                hit = arrivals[way][l] == b
-                way_of = jnp.where(hit, way, way_of)
-                lane_of = jnp.where(hit, l, lane_of)
-        target[q] = lax.select(at_home, own[index], arr[way_of, lane_of])
-
-    for q, b in enumerate(blocks_for(partner, rank_of, per_rank)):
-        gathered(b, q, pout)
-    handed = remote(pout, pin, fx_s, fx_r, partner)
-    handed.start()
-    for q, b in enumerate(blocks_for(me, rank_of, per_rank)):
-        gathered(b, q, fin)
-
-    @pl.when(core == 0)
-    def _():
-        pltpu.make_async_copy(fin, newk, out_s.at[0]).start()
-
-    @pl.when(core == 1)
-    def _():
-        pltpu.make_async_copy(fin, newv, out_s.at[0]).start()
-
     handed.wait_recv()
 
-    @pl.when(core == 0)
-    def _():
-        pltpu.make_async_copy(pin, newv, out_s.at[1]).start()
-
-    @pl.when(core == 1)
-    def _():
-        pltpu.make_async_copy(pin, newk, out_s.at[1]).start()
-
     handed.wait_send()
-    arrived.wait_send()
     s1_o.wait_send()
     s1_l.wait_send()
     for copy in s2:
         copy.wait_send()
-    for off in range(2 * chips - 1):
-        remote(q_ref, qg.at[mine], q_s.at[off], q_r.at[mine], partner).wait_send()
     for l in range(2):
         @pl.when(l < chip_blocks * (near + 1))
         def _():
@@ -406,17 +368,28 @@
 
         lax.fori_loop(0, lanes, sent, 0)
 
-    pltpu.make_async_copy(fin, newk, out_s.at[0]).wait()
-    pltpu.make_async_copy(pin, newv, out_s.at[1]).wait()
-
-
-def load_kernel(chips, chip_blocks, rank_slots, steps, spill, pick, box, send, recv):
+    pltpu.make_async_copy(fin, newk, out_s).wait()
+
+
+def load_kernel(
+    chips, chip_blocks, rank_slots, steps, spill, q_in, pk, pv, pick, qg, other,
+    box, q_wide, q_ref, send, recv, q_s, q_r, ex_s, ex_r,
+):
     groups = lax.axis_size("grp")
     mine = lax.axis_index("grp")
+    me = lax.axis_index("blk")
+    z = me // 2
+    core = lax.rem(me, 2)
+    partner = 2 * z + 1 - core
+    rows_here = q_in.shape[0]
     barrier = pltpu.get_barrier_semaphore()
+    pl.semaphore_signal(barrier, inc=1, device_id={"blk": partner}, device_id_type=MESH)
     for off in range(1, groups):
-        peer = lax.rem(mine + off, groups)
-        pl.semaphore_signal(barrier, inc=1, device_id={"grp": peer}, device_id_type=MESH)
+        pl.semaphore_signal(barrier, inc=1, device_id={"grp": lax.rem(mine + off, groups)}, device_id_type=MESH)
+    for off in range(1, chips):
+        peer = 2 * lax.rem(z + off, chips) + core
+        pl.semaphore_signal(barrier, inc=1, device_id={"blk": peer}, device_id_type=MESH)
+
     chip_of = [spill[b] // (2 * rank_slots) for b in range(chips * chip_blocks)]
     load = jnp.int32(0)
     for n in range(chips - 1):
@@ -425,7 +398,15 @@
             crossing = crossing + (chip_of[b] > n).astype(jnp.int32)
         load = jnp.maximum(load, crossing)
     box[mine] = jnp.full(box.shape[1:], load, jnp.int32)
-    pl.semaphore_wait(barrier, groups - 1)
+    q_wide[...] = jnp.zeros_like(q_wide)
+    q_rows = q_in[...].astype(jnp.float32)
+    for h in range(KV):
+        for j in range(GROUPS * rows_here):
+            head = h * GROUPS + j // rows_here
+            i = j % rows_here
+            q_wide[h, j : j + 1, :] = q_rows[i : i + 1, head * HEAD : (head + 1) * HEAD]
+    q_ref[...] = q_wide[...].astype(jnp.bfloat16)
+    pl.semaphore_wait(barrier, groups + chips - 1)
 
     def copy_to(off, source):
         return pltpu.make_async_remote_copy(
@@ -433,8 +414,31 @@
             device_id={"grp": lax.rem(mine + off, groups)}, device_id_type=MESH,
         )
 
+    def remote(src, dst, s, r, rank):
+        return pltpu.make_async_remote_copy(
+            src_ref=src, dst_ref=dst, send_sem=s, recv_sem=r, device_id={"blk": rank}, device_id_type=MESH
+        )
+
     for off in range(1, groups):
         copy_to(off, mine).start()
+    slot = core * chips + z
+    q_copies = []
+    for off in range(1, chips):
+        peer = 2 * lax.rem(z + off, chips) + core
+        q_copies.append(remote(q_ref, qg.at[slot], q_s.at[off], q_r.at[slot], peer))
+    q_copies.append(remote(q_ref, qg.at[slot], q_s.at[0], q_r.at[slot], partner))
+    for copy in q_copies:
+        copy.start()
+
+    @pl.when(core == 0)
+    def _():
+        remote(pv, other, ex_s, ex_r, partner).start()
+
+    @pl.when(core == 1)
+    def _():
+        remote(pk, other, ex_s, ex_r, partner).start()
+
+    qg[slot] = q_ref[...]
     for off in range(1, groups):
         copy_to(off, lax.rem(mine + off, groups)).wait_recv()
     largest = jnp.max(box[...])
@@ -442,6 +446,19 @@
     for step in steps[:-1]:
         choice = choice + (largest > step).astype(jnp.int32)
     pick[0] = choice
+    for off in range(1, chips):
+        came = core * chips + lax.rem(z + off, chips)
+        remote(q_ref, qg.at[came], q_s.at[0], q_r.at[came], partner).wait_recv()
+        q_copies.append(remote(qg.at[came], qg.at[came], q_s.at[chips - 1 + off], q_r.at[came], partner))
+        q_copies[-1].start()
+    exchanged = remote(pk, other, ex_s, ex_r, partner)
+    exchanged.wait_recv()
+    for zz in range(chips):
+        came = (1 - core) * chips + zz
+        remote(q_ref, qg.at[came], q_s.at[0], q_r.at[came], partner).wait_recv()
+    exchanged.wait_send()
+    for copy in q_copies:
+        copy.wait_send()
     for off in range(1, groups):
         copy_to(off, mine).wait_send()
 
@@ -510,7 +527,7 @@
                 jax.ShapeDtypeStruct((per_rank, *block), bf),
                 jax.ShapeDtypeStruct((per_rank, *block), bf),
             ),
-            in_specs=[smem_spec, vmem_spec, smem_spec, vmem_spec] + [any_spec] * 4,
+            in_specs=[smem_spec, vmem_spec, smem_spec, vmem_spec] + [any_spec] * 5,
             out_specs=(vmem_spec, any_spec, any_spec),
             scratch_shapes=[
                 vmem((blocks, *block), bf),
@@ -520,8 +537,6 @@
                 vmem((2, lanes, *block), bf),
                 vmem((per_rank, *block), bf),
                 vmem((per_rank, *block), bf),
-                vmem((per_rank, *block), bf),
-                vmem((ranks, KV, ROWS, HEAD), bf),
                 vmem((ranks * ROWS, blocks * tokens), f32),
                 vmem((ranks, KV, ROWS, HEAD), f32),
                 vmem((ranks, ROWS, HEAD), f32),
@@ -532,14 +547,8 @@
                 vmem((chips, KV, ROWS, HEAD), bf),
                 vmem((chips, ROWS, HEAD), f32),
                 pltpu.SMEM((2, lanes), jnp.int32),
-                vmem((KV, ROWS, HEAD), f32),
-                vmem((KV, ROWS, HEAD), bf),
                 vmem(queries.shape, f32),
-                dma((5,)),
-                dma,
-                dma,
-                dma((2 * chips - 1,)),
-                dma((ranks,)),
+                dma((6,)),
                 dma((2, lanes, PIECES)),
                 dma((2, lanes, PIECES)),
                 dma((2,)),
@@ -548,7 +557,7 @@
                 dma((2, chips)),
                 dma,
                 dma,
-                dma((2,)),
+                dma,
             ],
             compiler_params=pltpu.CompilerParams(
                 collective_id=1 + number, has_side_effects=True, vmem_limit_bytes=VMEM_BYTES
@@ -556,23 +565,36 @@
             name="exchange",
         )(*operands)
 
-    pick = pl.pallas_call(
+    pick, gathered_queries, other = pl.pallas_call(
         functools.partial(load_kernel, chips, chip_blocks, rank_slots, choices),
-        out_shape=jax.ShapeDtypeStruct((1,), jnp.int32),
-        in_specs=[smem_spec],
-        out_specs=smem_spec,
+        out_shape=(
+            jax.ShapeDtypeStruct((1,), jnp.int32),
+            jax.ShapeDtypeStruct((ranks, KV, ROWS, HEAD), bf),
+            jax.ShapeDtypeStruct((per_rank, *block), bf),
+        ),
+        in_specs=[smem_spec, vmem_spec, any_spec, any_spec],
+        out_specs=(smem_spec, vmem_spec, vmem_spec),
         scratch_shapes=[
             vmem((lax.axis_size("grp"), 8, HEAD), jnp.int32),
+            vmem((KV, ROWS, HEAD), f32),
+            vmem((KV, ROWS, HEAD), bf),
             dma((lax.axis_size("grp"),)),
             dma((lax.axis_size("grp"),)),
+            dma((2 * chips - 1,)),
+            dma((ranks,)),
+            dma,
+            dma,
         ],
-        compiler_params=pltpu.CompilerParams(collective_id=0, has_side_effects=True),
+        compiler_params=pltpu.CompilerParams(
+            collective_id=0, has_side_effects=True, vmem_limit_bytes=VMEM_BYTES
+        ),
         name="load",
-    )(spill_slots)
+    )(spill_slots, queries, prefill_keys, prefill_values)
     att, newk, newv = lax.switch(
         pick[0],
         [functools.partial(exchange, number, lanes) for number, lanes in enumerate(choices)],
-        context_lengths, block_table, spill_slots, queries, prefill_keys, prefill_values, cache_keys, pool_values_prior,
+        context_lengths, block_table, spill_slots, gathered_queries, other,
+        prefill_keys, prefill_values, cache_keys, pool_values_prior,
     )
 
     pool_keys, pool_values, att = pl.pallas_call(

time: 66.6 us -> 64.6 us (0.970)
  Pallas kernels: 64.6 us -> 62.2 us
    pallas_call x1, Pallas kernels: 52.2 us -> 45.5 us  [exchange(): pl.pallas_call(functools.partial(exchange_kernel, chips, lanes), out_shap...]
    pallas_call x1, Pallas kernels: 7.59 us -> 11.8 us  [per_device(): pl.pallas_call(functools.partial(load_kernel, chips, chip_blocks, rank_sl...]
where the time goes in v4:
time: 64.6 us; the launch traced here: 63.8 us
  Pallas kernels  62.2 us (96%)
  between operations  1.39 us (2%)
    pallas_call x1, Pallas kernels, exchange(): pl.pallas_call(functools.partial(exchange_kernel, chips, lanes), out_shap...  45.5 us
    pallas_call x1, Pallas kernels, per_device(): pl.pallas_call(functools.partial(load_kernel, chips, chip_blocks, rank_sl...  11.8 us
    pallas_call x1, Pallas kernels, per_device(): pl.pallas_call(place_kernel, out_shape=(jax.ShapeDtypeStruct(cache_keys.s...  4.88 us

profile of v4, /device:TPU:0, one launch (start us, length us, event | category | flops | bytes accessed | tf_op | source)
XLA Modules:
  0.0 63.8 jit_solution(12682155093350564777)
XLA Ops:
  0.6 11.8 %load.1 = (s32[1]{0:T(128)}, bf16[8,8,16,128]{3,2,1,0:T(8,128)(2,1)S(1)}, bf16[2,128,1024]{2,1,0:T(8,128)(2,1)S(1)}) custom-call(s32[16]{0:T(128)} %spill.3, bf16[2,5120]{1,0:T(2,128)(2,1)} %q_in.1, bf16[2,128,1024]{2,1,0:T(8,128)(2,1)} %pk.1, bf16[2,128,1024]{2,1,0:T(8,128)(2,1)} %pv.1), custom_call_target="tpu_custom_call" | custom-call | tf_op jit(solution)/shard_map/load/pallas_call | solution.py:568
  13.0 45.8 %conditional.1 = ((bf16[2,5120]{1,0:T(2,128)(2,1)S(1)}, bf16[2,128,1024]{2,1,0:T(8,128)(2,1)S(1)}, bf16[2,128,1024]{2,1,0:T(8,128)(2,1)S(1)})) conditional(s32[]{:T(128)} %bitcast.1, (s32[4]{0:T(128)}, s32[4,16]{1,0:T(4,128)}, s32[16]{0:T(128)}, bf16[8,8,16,128]{3,2,1,0:T(8,128)(2,1)S(1)}, ...), branch_computations={%region_0.0_spmd, %region_1.0_spmd, %region_2.0_spmd, %region_3.0_... | conditional | bytes 8 | solution.py:593
  13.0 45.5 %exchange.4 = (bf16[2,5120]{1,0:T(2,128)(2,1)S(1)}, bf16[2,128,1024]{2,1,0:T(8,128)(2,1)S(1)}, bf16[2,128,1024]{2,1,0:T(8,128)(2,1)S(1)}) custom-call(s32[4]{0:T(128)} %get-tuple-element.72.lengths, s32[4,16]{1,0:T(4,128)} %get-tuple-element.73.table, s32[16]{0:T(128)} %get-tuple-element.74.spill, bf16[8,8,16,128]{3,2,1,0:T(8,128)(2,1)S(1)} %get-tuple-element.75.qg, ...), custom_call_target="tpu_custom_call" | custom-call | tf_op jit(solution)/shard_map/cond/branch_0_fun/exchange/pallas_call | solution.py:523
  58.8 4.9 %place.1 = (bf16[8,128,1024]{2,1,0:T(8,128)(2,1)}, bf16[8,128,1024]{2,1,0:T(8,128)(2,1)}, bf16[2,5120]{1,0:T(2,128)(2,1)}) custom-call(s32[16]{0:T(128)} %spill.3, s32[1]{0:T(128)} %bitcast.first_ref, bf16[8,128,1024]{2,1,0:T(8,128)(2,1)} %ck.1, bf16[8,128,1024]{2,1,0:T(8,128)(2,1)} %cv.1, bf16[2,128,1024]{2,1,0:T(8,128)(2,1)S(1)} %get-tuple-element.123.newk, ...), custom_call_target="tpu_custom_call" | custom-call | tf_op jit(solution)/shard_map/place/pallas_call | solution.py:600

commit v5 on v4

--- a/solution.py
+++ b/solution.py
@@ -15,7 +15,7 @@
 REQ = 4
 ROWS = 16
 PIECES = 8
-HEADS_PER_STEP = 2
+HEADS_PER_STEP = 4
 LOW = -1e30
 FAR = 1 << 24
 VMEM_BYTES = 60 * 1024 * 1024
@@ -68,10 +68,10 @@
 
 
 def exchange_kernel(
-    chips, lanes, lengths, table, spill, qg, other, pk, pv, ck, cv,
+    chips, lanes, lengths, table, spill, q_half, other, pk, pv, ck, cv,
     att, newk, newv,
-    kall, vall, own, arr, snd, fin, pout, bias, part, lse, pin_o, pin_l, mo, ml, ro, rl, sched, att_wide,
-    loc, lane_s, lane_r, s1_s, s1_r, s2_s, s2_r, fx_s, fx_r, out_s,
+    kall, vall, own, arr, snd, fin, pout, qg, bias, part, lse, pin_o, pin_l, mo, ml, ro, rl, sched, att_wide,
+    loc, q_s, q_r, lane_s, lane_r, s1_s, s1_r, s2_s, s2_r, fx_s, fx_r, out_s,
 ):
     rank_slots, tokens, width = ck.shape
     per_rank = pk.shape[0]
@@ -122,6 +122,9 @@
     pltpu.make_async_copy(pk, own_mine, loc.at[4]).wait()
     load_other.wait()
     pl.semaphore_wait(barrier, chips)
+    ours = pl.ds(core * chips, chips)
+    q_copy = remote(q_half, qg.at[ours], q_s, q_r, partner)
+    q_copy.start()
 
     low_half = z < chips // 2
     near = jnp.where(low_half, z, chips - 1 - z)
@@ -185,7 +188,7 @@
                 compose(far_way, l, p)
                 lane_copy(far_way, l, p, far_next).start()
 
-    def attend(h):
+    def attend(h, carry):
         cols = pl.ds(pl.multiple_of(h * HEAD, HEAD), HEAD)
         q = qg[:, h].reshape(2 * chips * ROWS, HEAD)
         k = kall[:, :, cols].reshape(blocks * tokens, HEAD)
@@ -200,8 +203,10 @@
         lane = lax.broadcasted_iota(jnp.int32, (2 * chips, ROWS, HEAD), 2)
         level = (m + jnp.log(total)).reshape(2 * chips, ROWS, 1)
         lse[...] = jnp.where(lane == h, level, lse[...])
+        return carry
 
     near_step(0)
+    qg[ours] = q_half[...]
 
     row_count = 2 * chips * ROWS
     row = lax.broadcasted_iota(jnp.int32, (row_count, HEAD), 0)
@@ -235,14 +240,14 @@
     load_vp.wait()
     load_kc.wait()
     load_vc.wait()
+    q_copy.wait()
 
     attending = KV // HEADS_PER_STEP
 
     def mixed(i, carry):
         near_step(i)
+        lax.fori_loop((i - 1) * HEADS_PER_STEP, i * HEADS_PER_STEP, attend, 0)
         far_step(i - 1)
-        for e in range(HEADS_PER_STEP):
-            attend((i - 1) * HEADS_PER_STEP + e)
         return carry
 
     lax.fori_loop(1, 1 + attending, mixed, 0)
@@ -253,11 +258,9 @@
     s1_o.start()
     s1_l.start()
     near_step(1 + attending)
-    far_step(attending)
     s1_o.wait_recv()
     s1_l.wait_recv()
 
-    ours = pl.ds(core * chips, chips)
     level_a, level_b = lse[ours], pin_l[...]
     top = jnp.maximum(level_a, level_b)
     ea, eb = jnp.exp(level_a - top), jnp.exp(level_b - top)
@@ -276,6 +279,7 @@
         copy.start()
     ro[z] = mo[z]
     rl[z] = ml[z]
+    far_step(attending)
 
     def moving(i, carry):
         near_step(i)
@@ -421,12 +425,10 @@
 
     for off in range(1, groups):
         copy_to(off, mine).start()
-    slot = core * chips + z
     q_copies = []
     for off in range(1, chips):
         peer = 2 * lax.rem(z + off, chips) + core
-        q_copies.append(remote(q_ref, qg.at[slot], q_s.at[off], q_r.at[slot], peer))
-    q_copies.append(remote(q_ref, qg.at[slot], q_s.at[0], q_r.at[slot], partner))
+        q_copies.append(remote(q_ref, qg.at[z], q_s.at[off], q_r.at[z], peer))
     for copy in q_copies:
         copy.start()
 
@@ -438,7 +440,7 @@
     def _():
         remote(pk, other, ex_s, ex_r, partner).start()
 
-    qg[slot] = q_ref[...]
+    qg[z] = q_ref[...]
     for off in range(1, groups):
         copy_to(off, lax.rem(mine + off, groups)).wait_recv()
     largest = jnp.max(box[...])
@@ -447,15 +449,10 @@
         choice = choice + (largest > step).astype(jnp.int32)
     pick[0] = choice
     for off in range(1, chips):
-        came = core * chips + lax.rem(z + off, chips)
-        remote(q_ref, qg.at[came], q_s.at[0], q_r.at[came], partner).wait_recv()
-        q_copies.append(remote(qg.at[came], qg.at[came], q_s.at[chips - 1 + off], q_r.at[came], partner))
-        q_copies[-1].start()
+        came = lax.rem(z + off, chips)
+        remote(q_ref, qg.at[came], q_s.at[off], q_r.at[came], partner).wait_recv()
     exchanged = remote(pk, other, ex_s, ex_r, partner)
     exchanged.wait_recv()
-    for zz in range(chips):
-        came = (1 - core) * chips + zz
-        remote(q_ref, qg.at[came], q_s.at[0], q_r.at[came], partner).wait_recv()
     exchanged.wait_send()
     for copy in q_copies:
         copy.wait_send()
@@ -537,6 +534,7 @@
                 vmem((2, lanes, *block), bf),
                 vmem((per_rank, *block), bf),
                 vmem((per_rank, *block), bf),
+                vmem((ranks, KV, ROWS, HEAD), bf),
                 vmem((ranks * ROWS, blocks * tokens), f32),
                 vmem((ranks, KV, ROWS, HEAD), f32),
                 vmem((ranks, ROWS, HEAD), f32),
@@ -549,6 +547,8 @@
                 pltpu.SMEM((2, lanes), jnp.int32),
                 vmem(queries.shape, f32),
                 dma((6,)),
+                dma,
+                dma,
                 dma((2, lanes, PIECES)),
                 dma((2, lanes, PIECES)),
                 dma((2,)),
@@ -569,7 +569,7 @@
         functools.partial(load_kernel, chips, chip_blocks, rank_slots, choices),
         out_shape=(
             jax.ShapeDtypeStruct((1,), jnp.int32),
-            jax.ShapeDtypeStruct((ranks, KV, ROWS, HEAD), bf),
+            jax.ShapeDtypeStruct((chips, KV, ROWS, HEAD), bf),
             jax.ShapeDtypeStruct((per_rank, *block), bf),
         ),
         in_specs=[smem_spec, vmem_spec, any_spec, any_spec],
@@ -580,8 +580,8 @@
             vmem((KV, ROWS, HEAD), bf),
             dma((lax.axis_size("grp"),)),
             dma((lax.axis_size("grp"),)),
-            dma((2 * chips - 1,)),
-            dma((ranks,)),
+            dma((chips,)),
+            dma((chips,)),
             dma,
             dma,
         ],

time: 64.6 us -> 68 us (1.053)
  Pallas kernels: 62.2 us -> 66.1 us
    pallas_call x1, Pallas kernels: 45.5 us -> 50.3 us  [exchange(): pl.pallas_call(functools.partial(exchange_kernel, chips, lanes), out_shap...]
    pallas_call x1, Pallas kernels: 11.8 us -> 10.9 us  [per_device(): pl.pallas_call(functools.partial(load_kernel, chips, chip_blocks, rank_sl...]
where the time goes in v5:
time: 68 us; the launch traced here: 67.7 us
  Pallas kernels  66.1 us (97%)
  between operations  1.39 us (2%)
    pallas_call x1, Pallas kernels, exchange(): pl.pallas_call(functools.partial(exchange_kernel, chips, lanes), out_shap...  50.3 us
    pallas_call x1, Pallas kernels, per_device(): pl.pallas_call(functools.partial(load_kernel, chips, chip_blocks, rank_sl...  10.9 us
    pallas_call x1, Pallas kernels, per_device(): pl.pallas_call(place_kernel, out_shape=(jax.ShapeDtypeStruct(cache_keys.s...  4.88 us

profile of v5, /device:TPU:0, one launch (start us, length us, event | category | flops | bytes accessed | tf_op | source)
XLA Modules:
  0.0 67.7 jit_solution(7869079295451179150)
XLA Ops:
  0.6 10.9 %load.1 = (s32[1]{0:T(128)}, bf16[4,8,16,128]{3,2,1,0:T(8,128)(2,1)S(1)}, bf16[2,128,1024]{2,1,0:T(8,128)(2,1)S(1)}) custom-call(s32[16]{0:T(128)} %spill.3, bf16[2,5120]{1,0:T(2,128)(2,1)} %q_in.1, bf16[2,128,1024]{2,1,0:T(8,128)(2,1)} %pk.1, bf16[2,128,1024]{2,1,0:T(8,128)(2,1)} %pv.1), custom_call_target="tpu_custom_call" | custom-call | tf_op jit(solution)/shard_map/load/pallas_call | solution.py:568
  12.1 50.5 %conditional.1 = ((bf16[2,5120]{1,0:T(2,128)(2,1)S(1)}, bf16[2,128,1024]{2,1,0:T(8,128)(2,1)S(1)}, bf16[2,128,1024]{2,1,0:T(8,128)(2,1)S(1)})) conditional(s32[]{:T(128)} %bitcast.1, (s32[4]{0:T(128)}, s32[4,16]{1,0:T(4,128)}, s32[16]{0:T(128)}, bf16[4,8,16,128]{3,2,1,0:T(8,128)(2,1)S(1)}, ...), branch_computations={%region_0.0_spmd, %region_1.0_spmd, %region_2.0_spmd, %region_3.0_... | conditional | bytes 8 | solution.py:593
  12.1 50.3 %exchange.5 = (bf16[2,5120]{1,0:T(2,128)(2,1)S(1)}, bf16[2,128,1024]{2,1,0:T(8,128)(2,1)S(1)}, bf16[2,128,1024]{2,1,0:T(8,128)(2,1)S(1)}) custom-call(s32[4]{0:T(128)} %get-tuple-element.81.lengths, s32[4,16]{1,0:T(4,128)} %get-tuple-element.82.table, s32[16]{0:T(128)} %get-tuple-element.83.spill, bf16[4,8,16,128]{3,2,1,0:T(8,128)(2,1)S(1)} %get-tuple-element.84.q_half, ...), custom_call_target="tpu_custom_call" | custom-call | tf_op jit(solution)/shard_map/cond/branch_1_fun/exchange/pallas_call | solution.py:520
  62.7 4.9 %place.1 = (bf16[8,128,1024]{2,1,0:T(8,128)(2,1)}, bf16[8,128,1024]{2,1,0:T(8,128)(2,1)}, bf16[2,5120]{1,0:T(2,128)(2,1)}) custom-call(s32[16]{0:T(128)} %spill.3, s32[1]{0:T(128)} %bitcast.first_ref, bf16[8,128,1024]{2,1,0:T(8,128)(2,1)} %ck.1, bf16[8,128,1024]{2,1,0:T(8,128)(2,1)} %cv.1, bf16[2,128,1024]{2,1,0:T(8,128)(2,1)S(1)} %get-tuple-element.123.newk, ...), custom_call_target="tpu_custom_call" | custom-call | tf_op jit(solution)/shard_map/place/pallas_call | solution.py:600

commit v6 on v5

--- a/solution.py
+++ b/solution.py
@@ -15,7 +15,7 @@
 REQ = 4
 ROWS = 16
 PIECES = 8
-HEADS_PER_STEP = 4
+HEADS_PER_STEP = 2
 LOW = -1e30
 FAR = 1 << 24
 VMEM_BYTES = 60 * 1024 * 1024
@@ -24,8 +24,8 @@
 
 def lane_plan(spill, chips, z, lanes, chip_blocks, rank_slots):
     total = chips * chip_blocks
-    rank_of = [spill[b] // rank_slots for b in range(total)]
-    chip_of = [r // 2 for r in rank_of]
+    rank_of = [lax.div(spill[b], jnp.int32(rank_slots)) for b in range(total)]
+    chip_of = [r >> 1 for r in rank_of]
     sends, arrivals = [], []
     for way in range(2):
         dest = chip_of if way == 0 else [chips - 1 - c for c in chip_of]
@@ -188,7 +188,7 @@
                 compose(far_way, l, p)
                 lane_copy(far_way, l, p, far_next).start()
 
-    def attend(h, carry):
+    def attend(h):
         cols = pl.ds(pl.multiple_of(h * HEAD, HEAD), HEAD)
         q = qg[:, h].reshape(2 * chips * ROWS, HEAD)
         k = kall[:, :, cols].reshape(blocks * tokens, HEAD)
@@ -203,18 +203,17 @@
         lane = lax.broadcasted_iota(jnp.int32, (2 * chips, ROWS, HEAD), 2)
         level = (m + jnp.log(total)).reshape(2 * chips, ROWS, 1)
         lse[...] = jnp.where(lane == h, level, lse[...])
-        return carry
 
     near_step(0)
     qg[ours] = q_half[...]
 
     row_count = 2 * chips * ROWS
     row = lax.broadcasted_iota(jnp.int32, (row_count, HEAD), 0)
-    slot, inner = row // ROWS, row % ROWS
-    rank_row = 2 * (slot % chips) + slot // chips
-    row_id = rank_row * rows_here + inner % rows_here
+    slot, inner = row >> (ROWS.bit_length() - 1), row & (ROWS - 1)
+    rank_row = 2 * (slot & (chips - 1)) + (slot >> (chips.bit_length() - 1))
+    row_id = rank_row * rows_here + (inner & (rows_here - 1))
     valid = inner < GROUPS * rows_here
-    step, request = row_id // REQ, row_id % REQ
+    step, request = row_id >> (REQ.bit_length() - 1), row_id & (REQ - 1)
     token = lax.broadcasted_iota(jnp.int32, (row_count, HEAD), 1)
     edge = jnp.where(valid, token + (STEPS - 1) - step, FAR).astype(jnp.float32)
     columns = table.shape[1]
@@ -246,8 +245,9 @@
 
     def mixed(i, carry):
         near_step(i)
-        lax.fori_loop((i - 1) * HEADS_PER_STEP, i * HEADS_PER_STEP, attend, 0)
         far_step(i - 1)
+        for e in range(HEADS_PER_STEP):
+            attend((i - 1) * HEADS_PER_STEP + e)
         return carry
 
     lax.fori_loop(1, 1 + attending, mixed, 0)
@@ -301,7 +301,7 @@
         lax.fori_loop(0, lanes, drain, 0)
 
     def gathered(b, q, target):
-        at_home = b // chip_blocks == z
+        at_home = lax.div(b, jnp.int32(chip_blocks)) == z
         index = jnp.clip(b - z * chip_blocks, 0, chip_blocks - 1)
         way_of, lane_of = jnp.int32(0), jnp.int32(0)
         for way in range(2):
@@ -394,7 +394,7 @@
         peer = 2 * lax.rem(z + off, chips) + core
         pl.semaphore_signal(barrier, inc=1, device_id={"blk": peer}, device_id_type=MESH)
 
-    chip_of = [spill[b] // (2 * rank_slots) for b in range(chips * chip_blocks)]
+    chip_of = [lax.div(spill[b], jnp.int32(2 * rank_slots)) for b in range(chips * chip_blocks)]
     load = jnp.int32(0)
     for n in range(chips - 1):
         crossing = jnp.int32(0)

time: 68 us -> 66 us (0.971)
  Pallas kernels: 66.1 us -> 63.5 us
    pallas_call x1, Pallas kernels: 50.3 us -> 47.7 us  [exchange(): pl.pallas_call(functools.partial(exchange_kernel, chips, lanes), out_shap...]
where the time goes in v6:
time: 66 us; the launch traced here: 65.1 us
  Pallas kernels  63.5 us (96%)
  between operations  1.39 us (2%)
    pallas_call x1, Pallas kernels, exchange(): pl.pallas_call(functools.partial(exchange_kernel, chips, lanes), out_shap...  47.7 us
    pallas_call x1, Pallas kernels, per_device(): pl.pallas_call(functools.partial(load_kernel, chips, chip_blocks, rank_sl...  10.9 us
    pallas_call x1, Pallas kernels, per_device(): pl.pallas_call(place_kernel, out_shape=(jax.ShapeDtypeStruct(cache_keys.s...  4.88 us

profile of v6, /device:TPU:0, one launch (start us, length us, event | category | flops | bytes accessed | tf_op | source)
XLA Modules:
  0.0 65.1 jit_solution(16931375221975013741)
XLA Ops:
  0.6 10.9 %load.1 = (s32[1]{0:T(128)}, bf16[4,8,16,128]{3,2,1,0:T(8,128)(2,1)S(1)}, bf16[2,128,1024]{2,1,0:T(8,128)(2,1)S(1)}) custom-call(s32[16]{0:T(128)} %spill.3, bf16[2,5120]{1,0:T(2,128)(2,1)} %q_in.1, bf16[2,128,1024]{2,1,0:T(8,128)(2,1)} %pk.1, bf16[2,128,1024]{2,1,0:T(8,128)(2,1)} %pv.1), custom_call_target="tpu_custom_call" | custom-call | tf_op jit(solution)/shard_map/load/pallas_call | solution.py:568
  12.1 47.9 %conditional.1 = ((bf16[2,5120]{1,0:T(2,128)(2,1)S(1)}, bf16[2,128,1024]{2,1,0:T(8,128)(2,1)S(1)}, bf16[2,128,1024]{2,1,0:T(8,128)(2,1)S(1)})) conditional(s32[]{:T(128)} %bitcast.1, (s32[4]{0:T(128)}, s32[4,16]{1,0:T(4,128)}, s32[16]{0:T(128)}, bf16[4,8,16,128]{3,2,1,0:T(8,128)(2,1)S(1)}, ...), branch_computations={%region_0.0_spmd, %region_1.0_spmd, %region_2.0_spmd, %region_3.0_... | conditional | bytes 8 | solution.py:593
  12.1 47.7 %exchange.5 = (bf16[2,5120]{1,0:T(2,128)(2,1)S(1)}, bf16[2,128,1024]{2,1,0:T(8,128)(2,1)S(1)}, bf16[2,128,1024]{2,1,0:T(8,128)(2,1)S(1)}) custom-call(s32[4]{0:T(128)} %get-tuple-element.81.lengths, s32[4,16]{1,0:T(4,128)} %get-tuple-element.82.table, s32[16]{0:T(128)} %get-tuple-element.83.spill, bf16[4,8,16,128]{3,2,1,0:T(8,128)(2,1)S(1)} %get-tuple-element.84.q_half, ...), custom_call_target="tpu_custom_call" | custom-call | tf_op jit(solution)/shard_map/cond/branch_1_fun/exchange/pallas_call | solution.py:520
  60.1 4.9 %place.1 = (bf16[8,128,1024]{2,1,0:T(8,128)(2,1)}, bf16[8,128,1024]{2,1,0:T(8,128)(2,1)}, bf16[2,5120]{1,0:T(2,128)(2,1)}) custom-call(s32[16]{0:T(128)} %spill.3, s32[1]{0:T(128)} %bitcast.first_ref, bf16[8,128,1024]{2,1,0:T(8,128)(2,1)} %ck.1, bf16[8,128,1024]{2,1,0:T(8,128)(2,1)} %cv.1, bf16[2,128,1024]{2,1,0:T(8,128)(2,1)S(1)} %get-tuple-element.123.newk, ...), custom_call_target="tpu_custom_call" | custom-call | tf_op jit(solution)/shard_map/place/pallas_call | solution.py:600
